TPU v7x, 512 devices: a whole 4x8x8 slice. The times are simulated.
512 devices in a mesh: grp: 16 (over z_hi, x), blk: 32 (over z_lo, y, core).
Axes of the slice: x: 4, y: 8, z: 8 (z_hi: 4, z_lo: 2; z = z_hi * 2 + z_lo), core: 2. Of those that a mesh axis runs over, the one named last changes fastest.
Arguments:
- src_embed: bfloat16 [262144, 256], P(('grp', 'blk')), may hold values from -1.5 to 1.5
- dst_embed: bfloat16 [262144, 256], P(('grp', 'blk')), may hold values from -1.5 to 1.5
- relation: float32 [1345, 256], replicated, may hold values from 0.1 to 1.9
- src_index: int32 [16, 32, 4, 512], P('grp', 'blk'), may hold values from 0 to 511
- dst_index: int32 [16, 32, 4, 512], P('grp', 'blk'), may hold values from 0 to 511
- rel_index: int32 [16, 32, 4, 512], P('grp', 'blk'), may hold values from 0 to 1344
- neg_index: int32 [16, 32, 4, 512], P('grp', 'blk'), may hold values from 0 to 511
- edge_count: int32 [16, 32, 4], P('grp', 'blk'), may hold values from 1 to 512, 1024 in all within a row
Outputs:
- grad_src: float32 [262144, 256], P(('grp', 'blk'))
- grad_dst: float32 [262144, 256], P(('grp', 'blk'))
- grad_rel: float32 [1345, 256], replicated
Inputs may be any that keep to these rules, and one draw needn't show every extreme that they name: `edge_count`: within one device's tiles the counts sum to 1024, and one tile of each device is full.
All inputs are finite; a program needn't handle non-finite values.
Results may differ from a plain program's by a relative error of at most 0.004.
Values may be sent and summed in bfloat16 or wider, within the bound.
A program may use at most 64 MiB of HBM per device.

v0:
```python
import jax
import jax.numpy as jnp
from jax import lax
from jax.sharding import PartitionSpec as P


def shifted(block, axis, distance):
    devices = range(lax.axis_size(axis))
    route = [((i - distance) % len(devices), i) for i in devices]
    return lax.ppermute(block, axis, route)


def one_hot_rows(indices, width, dtype):
    columns = jnp.arange(width, dtype=jnp.int32)
    return (indices[:, None] == columns[None, :]).astype(dtype)


def pick_rows(table, block):
    return jnp.dot(table, block, preferred_element_type=jnp.float32).astype(jnp.bfloat16)


def spread_rows(table, values):
    return lax.dot_general(
        table,
        values,
        (((0,), (0,)), ((), ())),
        precision=lax.Precision.HIGHEST,
        preferred_element_type=jnp.float32,
    )


def tile_terms(
    src_block, dst_block, relation, src_rows_idx, dst_rows_idx, rel_rows_idx, neg_rows_idx, count
):
    slots = src_rows_idx.shape[0]
    negatives = neg_rows_idx.shape[0]
    entities = src_block.shape[0]
    src_table = one_hot_rows(src_rows_idx, entities, jnp.bfloat16)
    dst_table = one_hot_rows(dst_rows_idx, entities, jnp.bfloat16)
    neg_table = one_hot_rows(neg_rows_idx, entities, jnp.bfloat16)
    src_rows = pick_rows(src_table, src_block)
    rel_rows = jnp.take(relation, rel_rows_idx, axis=0)
    query = (src_rows.astype(jnp.float32) * rel_rows).astype(jnp.bfloat16)
    dst_rows = pick_rows(dst_table, dst_block)
    neg_rows = pick_rows(neg_table, dst_block)
    positive = jnp.sum(query.astype(jnp.float32) * dst_rows.astype(jnp.float32), axis=1)
    scores = lax.dot_general(
        query, neg_rows, (((1,), (1,)), ((), ())), preferred_element_type=jnp.float32
    )
    live = (jnp.arange(slots, dtype=jnp.int32) < count).astype(jnp.float32)
    dpos = -live * jax.nn.sigmoid(-positive)
    dneg = (jax.nn.sigmoid(scores) * (live[:, None] / negatives)).astype(jnp.bfloat16)
    dquery = dpos[:, None] * dst_rows.astype(jnp.float32) + jnp.dot(
        dneg, neg_rows, preferred_element_type=jnp.float32
    )
    neg_grad = lax.dot_general(
        dneg, query, (((0,), (0,)), ((), ())), preferred_element_type=jnp.float32
    )
    grad_src = spread_rows(src_table.astype(jnp.float32), dquery * rel_rows)
    grad_dst = spread_rows(dst_table.astype(jnp.float32), dpos[:, None] * query.astype(jnp.float32))
    grad_dst = grad_dst + spread_rows(neg_table.astype(jnp.float32), neg_grad)
    grad_rel = (
        jnp.zeros(relation.shape, jnp.float32)
        .at[rel_rows_idx]
        .add(dquery * src_rows.astype(jnp.float32))
    )
    return (grad_src, grad_dst, grad_rel)


def body(src_embed, dst_embed, relation, src_index, dst_index, rel_index, neg_index, edge_count):
    steps = src_index.shape[2]
    block = dst_embed
    grad_src = jnp.zeros(src_embed.shape, jnp.float32)
    rel_total = jnp.zeros(relation.shape, jnp.float32)
    carried = jnp.zeros(dst_embed.shape, jnp.float32)
    for step in range(steps):
        if step > 0:
            block = shifted(block, "blk", 1)
            carried = shifted(carried, "blk", 1)
        part_src, part_dst, rel_part = tile_terms(
            src_embed,
            block,
            relation,
            src_index[0, 0, step],
            dst_index[0, 0, step],
            rel_index[0, 0, step],
            neg_index[0, 0, step],
            edge_count[0, 0, step],
        )
        grad_src = grad_src + part_src
        rel_total = rel_total + rel_part
        carried = carried + part_dst
    grad_dst = shifted(carried, "blk", 1 - steps)
    grad_rel = lax.psum(rel_total, ("grp", "blk"))
    return (grad_src, grad_dst, grad_rel)


def solution(mesh):
    in_specs = (
        P(("grp", "blk"), None),
        P(("grp", "blk"), None),
        P(),
        P("grp", "blk", None, None),
        P("grp", "blk", None, None),
        P("grp", "blk", None, None),
        P("grp", "blk", None, None),
        P("grp", "blk", None),
    )
    out_specs = (P(("grp", "blk"), None), P(("grp", "blk"), None), P())
    return jax.shard_map(body, mesh=mesh, in_specs=in_specs, out_specs=out_specs, check_vma=False)
```

profile of v0, /device:TPU:1, one launch (start us, length us, event | category | flops | bytes accessed | tf_op | source)
XLA Modules:
  0.0 400.3 jit_solution(8964057643239246085)
XLA Ops:
  7.2 4.7 %collective-permute-start = (bf16[512,256]{1,0:T(8,128)(2,1)}, bf16[512,256]{1,0:T(8,128)(2,1)}, u32[]{:S(2)}, u32[]{:S(2)}) collective-permute-start(bf16[512,256]{1,0:T(8,128)(2,1)} %param.11), channel_id=1, source_target_pairs={{31,0},{0,1},{1,2},{2,3},{3,4},{4,5},{5,6},{6,7},{7,8},{8,9},{9,10... | collective-permute-start | bytes 786440 | tf_op jit(solution)/shard_map/ppermute | solution.py:10
  12.9 1.4 fusion.111
  14.3 1.5 fusion.109
  15.8 1.4 fusion.108
  17.2 1.3 convolution_convert_fusion.9
  18.5 1.4 fusion.112
  20.0 1.3 fusion.28
  21.3 1.6 gather_fusion
  24.4 1.2 fusion.40
  26.4 1.9 convolution_add_fusion.5
  28.4 2.1 collective-permute-start.3
  32.2 1.3 fusion.113
  33.5 2.2 gather_fusion.1
  35.7 1.2 fusion.26
  37.5 1.6 gather_fusion.2
  40.6 1.2 fusion.101
  41.8 1.6 gather_fusion.3
  45.0 1.2 fusion.100
  46.2 2.2 fusion.41
  48.5 1.4 fusion.46
  50.5 1.3 convolution_convert_fusion.6
  53.4 2.0 convolution_add_fusion.6
  55.5 3.6 collective-permute-start.1
  59.0 1.1 fusion.115
  60.2 2.0 fusion.39
  62.2 7.9 %scatter_custom_fusion = f32[1345,256]{1,0:T(8,128)} fusion(s32[1024]{0:T(1024)S(1)} %bitcast.104, f32[512,256]{1,0:T(8,128)} %get-tuple-element.40, f32[]{:T(128)} %constant.35, f32[512,256]{1,0:T(8,128)} %get-tuple-element.42, f32[]{:T(128)} %constant.26.clone.1), kind=kCustom, calls=%fused_computation.60 | custom fusion | flops 524288 | bytes 2425864 | tf_op jit(solution)/shard_map/add | solution.py:91
  70.1 1.6 fusion.47
  72.4 3.0 fusion.20
  75.3 1.9 collective-permute-start.4
  77.3 1.3 convolution_convert_fusion.3
  80.6 3.6 collective-permute-start.2
  84.2 1.9 fusion.36
  86.3 4.6 %scatter_custom_fusion.1 = f32[1345,256]{1,0:T(8,128)} fusion(s32[512]{0:T(512)} %bitcast.105, f32[512,256]{1,0:T(8,128)S(1)} %copy.19, f32[]{:T(128)} %constant.26.clone.1), kind=kCustom, calls=%fused_computation.85 | custom fusion | flops 131072 | bytes 1377792 | tf_op jit(solution)/shard_map/scatter-add | solution.py:65
  90.9 2.0 add.175
  93.9 1.3 convolution_convert_fusion
  95.2 1.5 fusion.48
  97.9 1.3 fusion.98
  99.2 2.0 add.168
  101.3 1.9 collective-permute-start.5
  105.3 4.5 %scatter_fusion = f32[1345,256]{1,0:T(8,128)S(1)} fusion(f32[1345,256]{1,0:T(8,128)S(1)} %add.175, s32[512]{0:T(512)} %bitcast.93, f32[512,256]{1,0:T(8,128)} %copy.20), kind=kCustom, calls=%fused_computation.6 | custom fusion | flops 131072 | bytes 1574912 | tf_op jit(solution)/shard_map/scatter-add | solution.py:65
  111.3 1.8 fusion.33
  113.1 1.7 convolution_add_fusion
  114.8 1.2 add.170
  116.0 6.7 %collective-permute-start.6 = (f32[512,256]{1,0:T(8,128)S(1)}, f32[512,256]{1,0:T(8,128)S(1)}, u32[]{:S(2)}, u32[]{:S(2)}) collective-permute-start(f32[512,256]{1,0:T(8,128)S(1)} %add.170), channel_id=1, source_target_pairs={{3,0},{4,1},{5,2},{6,3},{7,4},{8,5},{9,6},{10,7},{11,8},{12,9},{13... | collective-permute-start | bytes 1572872 | tf_op jit(solution)/shard_map/ppermute | solution.py:10
  123.8 1.7 convolution_add_fusion.2
  125.5 13.7 %collective-permute-done.6 = f32[512,256]{1,0:T(8,128)S(1)} collective-permute-done((f32[512,256]{1,0:T(8,128)S(1)}, f32[512,256]{1,0:T(8,128)S(1)}, u32[]{:S(2)}, u32[]{:S(2)}) %collective-permute-start.6) | collective-permute-done | bytes 524320 | tf_op jit(solution)/shard_map/ppermute | solution.py:10
  139.2 251.0 %all-reduce.2.cloned.1.call-done = f32[1345,256]{1,0:T(8,128)} async-done(((f32[1345,256]{1,0:T(8,128)}), f32[1345,256]{1,0:T(8,128)}) %all-reduce.2.cloned.1.call-update) | async-done | bytes 1377296 | tf_op jit(solution)/shard_map/psum | solution.py:94
  390.9 2.5 copy.27
  (149 shorter events, 21.1 us)
Async XLA Ops:
  7.2 14.1 %copy-start = (f32[1345,256]{1,0:T(8,128)S(1)}, f32[1345,256]{1,0:T(8,128)}, u32[]{:S(2)}) copy-start(f32[1345,256]{1,0:T(8,128)} %param.12) | copy-start | bytes 4131844
  7.2 383.0 %all-reduce.2.cloned.1.call-start = ((), (), s32[]{:S(2)}) async-start(), calls=%async_computation | async-start | bytes 2768896 | tf_op jit(solution)/shard_map/psum | solution.py:94
  7.2 41.2 %collective-permute-start = (bf16[512,256]{1,0:T(8,128)(2,1)}, bf16[512,256]{1,0:T(8,128)(2,1)}, u32[]{:S(2)}, u32[]{:S(2)}) collective-permute-start(bf16[512,256]{1,0:T(8,128)(2,1)} %param.11), channel_id=1, source_target_pairs={{31,0},{0,1},{1,2},{2,3},{3,4},{4,5},{5,6},{6,7},{7,8},{8,9},{9,10... | collective-permute-start | bytes 786440 | tf_op jit(solution)/shard_map/ppermute | solution.py:10
  12.8 10.0 %copy-start.43 = (pred[512]{0:T(512)(128)(4,1)}, pred[512]{0:T(512)(128)(4,1)S(1)}, u32[]{:S(2)}) copy-start(pred[512]{0:T(512)(128)(4,1)S(1)} %compare_and_fusion.3) | copy-start | bytes 1540
  14.3 5.7 %copy-start.31 = (s32[1,1,1,512]{3,2,1,0:T(1,128)}, s32[1,1,1,512]{3,2,1,0:T(1,128)S(1)}, u32[]{:S(2)}) copy-start(s32[1,1,1,512]{3,2,1,0:T(1,128)S(1)} %get-tuple-element.30) | copy-start | bytes 6148
  14.3 21.4 %copy-start.37 = (s32[1,1,1,512]{3,2,1,0:T(1,128)}, s32[1,1,1,512]{3,2,1,0:T(1,128)S(1)}, u32[]{:S(2)}) copy-start(s32[1,1,1,512]{3,2,1,0:T(1,128)S(1)} %get-tuple-element.29) | copy-start | bytes 6148
  14.3 25.8 %copy-start.35 = (s32[1,1,1,512]{3,2,1,0:T(1,128)}, s32[1,1,1,512]{3,2,1,0:T(1,128)S(1)}, u32[]{:S(2)}) copy-start(s32[1,1,1,512]{3,2,1,0:T(1,128)S(1)} %get-tuple-element.31) | copy-start | bytes 6148
  26.1 5.5 %copy-start.22 = (s32[1,1,4,512]{3,2,1,0:T(4,128)S(1)}, s32[1,1,4,512]{3,2,1,0:T(4,128)}, u32[]{:S(2)}) copy-start(s32[1,1,4,512]{3,2,1,0:T(4,128)} %param.15) | copy-start | bytes 24580
  28.4 44.0 %collective-permute-start.3 = (f32[512,256]{1,0:T(8,128)}, f32[512,256]{1,0:T(8,128)}, u32[]{:S(2)}, u32[]{:S(2)}) collective-permute-start(f32[512,256]{1,0:T(8,128)} %convolution_add_fusion.5), channel_id=1, source_target_pairs={{31,0},{0,1},{1,2},{2,3},{3,4},{4,5},{5,6},{6,7},{7,8},{8,9},{9,10... | collective-permute-start | bytes 1572872 | tf_op jit(solution)/shard_map/ppermute | solution.py:10
  33.5 2.2 copy-start.12
  41.8 2.6 copy-start.33
  43.4 2.8 copy-start.32
  43.4 2.8 copy-start.44
  44.4 4.0 %copy-start.2 = (f32[512,256]{1,0:T(8,128)S(1)}, f32[512,256]{1,0:T(8,128)}, u32[]{:S(2)}) copy-start(f32[512,256]{1,0:T(8,128)} %fusion.26) | copy-start | bytes 1572868
  44.4 4.0 %copy-start.7 = (f32[512,256]{1,0:T(8,128)S(1)}, f32[512,256]{1,0:T(8,128)}, u32[]{:S(2)}) copy-start(f32[512,256]{1,0:T(8,128)} %gather_fusion.1) | copy-start | bytes 1572868
  44.4 4.0 %copy-start.42 = (s32[1,1,1,512]{3,2,1,0:T(1,128)S(1)}, s32[1,1,1,512]{3,2,1,0:T(1,128)}, u32[]{:S(2)}) copy-start(s32[1,1,1,512]{3,2,1,0:T(1,128)} %get-tuple-element.21) | copy-start | bytes 6148
  55.5 14.6 %collective-permute-start.1 = (bf16[512,256]{1,0:T(8,128)(2,1)}, bf16[512,256]{1,0:T(8,128)(2,1)}, u32[]{:S(2)}, u32[]{:S(2)}) collective-permute-start(bf16[512,256]{1,0:T(8,128)(2,1)} %collective-permute-done), channel_id=1, source_target_pairs={{31,0},{0,1},{1,2},{2,3},{3,4},{4,5},{5,6},{6,7},{7,8},{8,9},{9,10... | collective-permute-start | bytes 786440 | tf_op jit(solution)/shard_map/ppermute | solution.py:10
  62.2 7.9 %copy-start.10 = (f32[512,256]{0,1:T(8,128)S(1)}, f32[512,256]{0,1:T(8,128)}, u32[]{:S(2)}) copy-start(f32[512,256]{0,1:T(8,128)} %copy.15) | copy-start | bytes 1572868
  62.2 7.9 %copy-start.29 = (s32[1,1,1,512]{3,2,1,0:T(1,128)S(1)}, s32[1,1,1,512]{3,2,1,0:T(1,128)}, u32[]{:S(2)}) copy-start(s32[1,1,1,512]{3,2,1,0:T(1,128)} %get-tuple-element.23) | copy-start | bytes 6148
  62.2 7.9 %copy-start.47 = (pred[512]{0:T(512)(128)(4,1)S(1)}, pred[512]{0:T(512)(128)(4,1)}, u32[]{:S(2)}) copy-start(pred[512]{0:T(512)(128)(4,1)} %compare_and_fusion.1) | copy-start | bytes 1540
  70.0 2.3 copy-start.13
  70.1 2.3 copy-start.20
  71.6 7.8 %copy-start.3 = (f32[512,256]{0,1:T(8,128)}, f32[512,256]{0,1:T(8,128)S(1)}, u32[]{:S(2)}) copy-start(f32[512,256]{0,1:T(8,128)S(1)} %get-tuple-element.38) | copy-start | bytes 1572868
  71.7 5.6 %copy-start.40 = (s32[1,1,1,512]{3,2,1,0:T(1,128)S(1)}, s32[1,1,1,512]{3,2,1,0:T(1,128)}, u32[]{:S(2)}) copy-start(s32[1,1,1,512]{3,2,1,0:T(1,128)} %get-tuple-element.19) | copy-start | bytes 6148
  72.3 7.1 %copy-start.23 = (f32[512]{0:T(512)}, f32[512]{0:T(512)S(1)}, u32[]{:S(2)}) copy-start(f32[512]{0:T(512)S(1)} %divide_multiply_fusion.1) | copy-start | bytes 6148
  72.4 6.2 %copy-start.50 = (f32[512]{0:T(512)S(1)}, f32[512]{0:T(512)}, u32[]{:S(2)}) copy-start(f32[512]{0:T(512)} %fusion.101) | copy-start | bytes 6148
  75.3 23.9 %collective-permute-start.4 = (f32[512,256]{1,0:T(8,128)}, f32[512,256]{1,0:T(8,128)}, u32[]{:S(2)}, u32[]{:S(2)}) collective-permute-start(f32[512,256]{1,0:T(8,128)} %fusion.20), channel_id=1, source_target_pairs={{31,0},{0,1},{1,2},{2,3},{3,4},{4,5},{5,6},{6,7},{7,8},{8,9},{9,10... | collective-permute-start | bytes 1572872 | tf_op jit(solution)/shard_map/ppermute | solution.py:10
  80.6 13.2 %collective-permute-start.2 = (bf16[512,256]{1,0:T(8,128)(2,1)}, bf16[512,256]{1,0:T(8,128)(2,1)}, u32[]{:S(2)}, u32[]{:S(2)}) collective-permute-start(bf16[512,256]{1,0:T(8,128)(2,1)} %collective-permute-done.1), channel_id=1, source_target_pairs={{31,0},{0,1},{1,2},{2,3},{3,4},{4,5},{5,6},{6,7},{7,8},{8,9},{9,10... | collective-permute-start | bytes 786440 | tf_op jit(solution)/shard_map/ppermute | solution.py:10
  90.9 2.9 copy-start.39
  93.0 2.2 copy-start.8
  93.0 2.2 copy-start.28
  93.9 2.8 copy-start.49
  99.2 5.1 %copy-start.14 = (f32[512,256]{0,1:T(8,128)S(1)}, f32[512,256]{0,1:T(8,128)}, u32[]{:S(2)}) copy-start(f32[512,256]{0,1:T(8,128)} %get-tuple-element.46) | copy-start | bytes 1572868
  101.3 13.5 %collective-permute-start.5 = (f32[512,256]{1,0:T(8,128)}, f32[512,256]{1,0:T(8,128)}, u32[]{:S(2)}, u32[]{:S(2)}) collective-permute-start(f32[512,256]{1,0:T(8,128)} %add.168), channel_id=1, source_target_pairs={{31,0},{0,1},{1,2},{2,3},{3,4},{4,5},{5,6},{6,7},{7,8},{8,9},{9,10... | collective-permute-start | bytes 1572872 | tf_op jit(solution)/shard_map/ppermute | solution.py:10
  113.0 9.7 %copy-start.4 = (f32[512,256]{0,1:T(8,128)S(1)}, f32[512,256]{0,1:T(8,128)}, u32[]{:S(2)}) copy-start(f32[512,256]{0,1:T(8,128)} %copy-done.3) | copy-start | bytes 1572868
  113.0 9.7 %copy-start.11 = (f32[512,256]{0,1:T(8,128)S(1)}, f32[512,256]{0,1:T(8,128)}, u32[]{:S(2)}) copy-start(f32[512,256]{0,1:T(8,128)} %copy.15) | copy-start | bytes 1572868
  113.1 9.7 %copy-start.15 = (f32[512,256]{0,1:T(8,128)S(1)}, f32[512,256]{0,1:T(8,128)}, u32[]{:S(2)}) copy-start(f32[512,256]{0,1:T(8,128)} %get-tuple-element.45) | copy-start | bytes 1572868
  113.1 9.7 %copy-start.19 = (f32[512,256]{1,0:T(8,128)S(1)}, f32[512,256]{1,0:T(8,128)}, u32[]{:S(2)}) copy-start(f32[512,256]{1,0:T(8,128)} %convolution_add_fusion.6) | copy-start | bytes 1572868
  113.1 9.7 %copy-start.25 = (f32[512]{0:T(512)S(1)}, f32[512]{0:T(512)}, u32[]{:S(2)}) copy-start(f32[512]{0:T(512)} %copy-done.23) | copy-start | bytes 6148
  113.1 9.7 %copy-start.36 = (s32[1,1,1,512]{3,2,1,0:T(1,128)S(1)}, s32[1,1,1,512]{3,2,1,0:T(1,128)}, u32[]{:S(2)}) copy-start(s32[1,1,1,512]{3,2,1,0:T(1,128)} %copy-done.35) | copy-start | bytes 6148
  113.1 9.7 %copy-start.48 = (pred[512]{0:T(512)(128)(4,1)S(1)}, pred[512]{0:T(512)(128)(4,1)}, u32[]{:S(2)}) copy-start(pred[512]{0:T(512)(128)(4,1)} %compare_and_fusion.1) | copy-start | bytes 1540
  116.0 7.8 %copy-start.6 = (f32[512,256]{0,1:T(8,128)S(1)}, f32[512,256]{0,1:T(8,128)}, u32[]{:S(2)}) copy-start(f32[512,256]{0,1:T(8,128)} %copy-done.5) | copy-start | bytes 1572868
  116.0 7.8 %copy-start.9 = (f32[512,256]{0,1:T(8,128)S(1)}, f32[512,256]{0,1:T(8,128)}, u32[]{:S(2)}) copy-start(f32[512,256]{0,1:T(8,128)} %copy.17) | copy-start | bytes 1572868
  116.0 7.8 %copy-start.16 = (f32[512,256]{0,1:T(8,128)S(1)}, f32[512,256]{0,1:T(8,128)}, u32[]{:S(2)}) copy-start(f32[512,256]{0,1:T(8,128)} %get-tuple-element.47) | copy-start | bytes 1572868
  116.0 7.8 %copy-start.27 = (f32[512]{0:T(512)S(1)}, f32[512]{0:T(512)}, u32[]{:S(2)}) copy-start(f32[512]{0:T(512)} %copy-done.26) | copy-start | bytes 6148
  116.0 7.8 %copy-start.34 = (s32[1,1,1,512]{3,2,1,0:T(1,128)S(1)}, s32[1,1,1,512]{3,2,1,0:T(1,128)}, u32[]{:S(2)}) copy-start(s32[1,1,1,512]{3,2,1,0:T(1,128)} %get-tuple-element.28) | copy-start | bytes 6148
  116.0 7.8 %copy-start.46 = (pred[512]{0:T(512)(128)(4,1)S(1)}, pred[512]{0:T(512)(128)(4,1)}, u32[]{:S(2)}) copy-start(pred[512]{0:T(512)(128)(4,1)} %compare_and_fusion) | copy-start | bytes 1540
  116.0 23.2 %collective-permute-start.6 = (f32[512,256]{1,0:T(8,128)S(1)}, f32[512,256]{1,0:T(8,128)S(1)}, u32[]{:S(2)}, u32[]{:S(2)}) collective-permute-start(f32[512,256]{1,0:T(8,128)S(1)} %add.170), channel_id=1, source_target_pairs={{3,0},{4,1},{5,2},{6,3},{7,4},{8,5},{9,6},{10,7},{11,8},{12,9},{13... | collective-permute-start | bytes 1572872 | tf_op jit(solution)/shard_map/ppermute | solution.py:10
  (11 other events, 18.1 us)
Sparse Core Ops, SparseCore 0:
  111.0 279.0 all-reduce.1
where the time goes:
time: 401 us; the launch traced here: 400 us
  waiting for transfers between devices  265 us (66%)
  matrix products  44.8 us (11%)
  other arithmetic  29.6 us (7%)
  starting transfers between devices  24.6 us (6%)
  local copies, waits for them, and re-layouts  21.7 us (5%)
  between operations  15 us (4%)
    psum x1, waiting for transfers between devices, body(): grad_rel = lax.psum(rel_total, ('grp', 'blk'))  251 us
    ppermute x7, starting transfers between devices, shifted(): return lax.ppermute(block, axis, route)  24.5 us
    dot_general x12, matrix products, spread_rows(): lax.dot_general(table, values, (((0,), (0,)), ((), ())), precision=lax.Pr...  21.1 us
    dot_general x12, matrix products, pick_rows(): jnp.dot(table, block, preferred_element_type=jnp.float32)  14 us
    ppermute x7, waiting for transfers between devices, shifted(): return lax.ppermute(block, axis, route)  13.7 us
    add x2, other arithmetic, body(): rel_total = rel_total + rel_part  9.88 us
    scatter-add x2, other arithmetic, tile_terms(): grad_rel = jnp.zeros(relation.shape, jnp.float32).at[rel_rows_idx].add(dq...  9.12 us
    gather x6, local copies, waits for them, and re-layouts, tile_terms(): rel_rows = jnp.take(relation, rel_rows_idx, axis=0)  8.96 us
  transfers between devices with their start and end apart: 8, of which 2 were waited for; matrix products, arithmetic and copies ran while one was open for 22% of the time, Pallas kernels for 0%

commit v1 on v0

v1 whole, which is shorter than its diff:
```python
import functools

import jax
import jax.numpy as jnp
from jax import lax
from jax.experimental import pallas as pl
from jax.experimental.pallas import tpu as pltpu
from jax.sharding import PartitionSpec as P

MESH = pl.DeviceIdType.MESH
F32 = jnp.float32
BF16 = jnp.bfloat16
NX = 4
NY = 8
ZLO = 2


def nt(a, b):
    return lax.dot_general(a, b, (((1,), (1,)), ((), ())), preferred_element_type=F32)


def nn(a, b):
    return jnp.dot(a, b, preferred_element_type=F32)


def kernel(
    nz, rels, rows_mm, chunk,
    src_hbm, dst_hbm, rel_hbm, si_hbm, di_hbm, ri_hbm, ni_hbm, ec_hbm,
    gs_out, gd_out, rel_out,
    part, src_v, src_far, rel_v, rel_pad, rel_t, src_t, idx, idx_far, ec, ec_far,
    ohs, ohr, sr, rr, qt, gw, gs, gr, gs_send, gs_recv, ga_send, ga_recv, gb_send, gb_recv,
    gh_send, gh_recv, half_recv, xs, x_recv, ys, y_recv, z_all, rel_all,
    in_sem, out_sem, part_send, part_recv, fwd_send, far_send, far_recv,
    g_send, g_recv, h_send, h_recv,
    xs_send, xs_recv, ys_send, ys_recv, zs_send, zs_recv,
    ya_send, ya_recv, xa_send, xa_recv, ca_send, ca_recv,
):
    ent, width = dst_hbm.shape
    half = width // 2
    xrows = NY * chunk
    nchip = ZLO * NY
    grp, blk = lax.axis_index("grp"), lax.axis_index("blk")
    core = lax.rem(blk, 2)
    chip = blk // 2
    y = lax.rem(chip, NY)
    z = (grp // NX) * ZLO + chip // NY
    x = lax.rem(grp, NX)
    even = core == 0
    nxt = lax.rem(chip + 1, nchip) * 2 + core
    prv = lax.rem(chip + nchip - 1, nchip) * 2 + core
    sib = (grp, chip * 2 + 1 - core)

    def at_x(i):
        return ((grp // NX) * NX + i, blk)

    def at_y(i):
        return (grp, (chip // NY) * NY * 2 + i * 2 + core)

    def at_z(i):
        return ((i // ZLO) * NX + x, lax.rem(i, ZLO) * NY * 2 + y * 2 + core)

    x_others = [lax.rem(x + k, NX) for k in range(1, NX)]
    y_others = [lax.rem(y + k, NY) for k in range(1, NY)]
    z_others = [lax.rem(z + k, nz) for k in range(1, nz)]

    def remote(source, target, send, recv, device):
        return pltpu.make_async_remote_copy(
            src_ref=source, dst_ref=target, send_sem=send, recv_sem=recv,
            device_id=device, device_id_type=MESH,
        )

    def arrived(target, recv):
        remote(target, target, recv, recv, sib).wait_recv()

    own = [(si_hbm, 0), (di_hbm, 1), (ri_hbm, 2), (ni_hbm, 3)]
    loads = [
        pltpu.make_async_copy(rel_hbm, rel_v, in_sem.at[0]),
        pltpu.make_async_copy(src_hbm, src_v, in_sem.at[1]),
        pltpu.make_async_copy(dst_hbm, part.at[0], in_sem.at[2]),
        pltpu.make_async_copy(ec_hbm, ec, in_sem.at[3]),
    ] + [pltpu.make_async_copy(ref, idx.at[k], in_sem.at[4 + k]) for ref, k in own]
    for load in loads:
        load.start()

    barrier = pltpu.get_barrier_semaphore()
    greet = [sib, (grp, nxt), (grp, prv)]
    greet += [at_x(i) for i in x_others] + [at_y(i) for i in y_others] + [at_z(i) for i in z_others]
    for device in greet:
        pl.semaphore_signal(barrier, inc=1, device_id=device, device_id_type=MESH)
    pl.semaphore_wait(barrier, len(greet))

    direct = 2 - core
    send_next = remote(
        dst_hbm, part.at[direct], part_send.at[0], part_recv.at[direct], (grp, nxt)
    )
    send_next.start()
    send_sib = remote(dst_hbm, part.at[3], part_send.at[1], part_recv.at[3], sib)
    far = [remote(src_hbm, src_far, far_send.at[0], far_recv.at[0], (grp, prv))]
    far += [remote(ec_hbm, ec_far, far_send.at[1], far_recv.at[1], (grp, prv))]
    far += [
        remote(ref, idx_far.at[k], far_send.at[2 + k], far_recv.at[2 + k], (grp, prv))
        for ref, k in own
    ]

    @pl.when(even)
    def _():
        send_sib.start()
        for copy in far:
            copy.start()

    for load in loads:
        load.wait()

    gr[...] = jnp.zeros_like(gr)
    rel_pad[...] = jnp.zeros_like(rel_pad)
    rel_pad[0:rels, :] = rel_v[...]
    turned = rel_pad[...].T
    high = turned.astype(BF16)
    rel_t[0:width, :] = high
    rel_t[width:, :] = (turned - high.astype(F32)).astype(BF16)
    src_t[...] = src_v[...].T

    def tile_of(w):
        if w in (0, 3):
            return w
        return jnp.where(even, 3 - w, w)

    def row_of(k, w):
        row = idx[k, pl.ds(tile_of(w), 1), :]
        if w == 3:
            row = jnp.where(even, idx_far[k, 3:4, :], row)
        return row

    def live_of(w):
        counts = ec[...].astype(F32)
        if w == 3:
            counts = jnp.where(even, ec_far[...].astype(F32), counts)
        place = lax.broadcasted_iota(jnp.int32, counts.shape, 1)
        count = jnp.sum(jnp.where(place == tile_of(w), counts, 0.0), axis=1, keepdims=True)
        slot = lax.broadcasted_iota(jnp.int32, (1, ent), 1).astype(F32)
        return (slot < count).astype(F32)

    def prepare(w):
        rows = lax.broadcasted_iota(jnp.int32, (ent, ent), 0)
        ohs[w] = (rows == row_of(0, w)).astype(BF16)
        rows = lax.broadcasted_iota(jnp.int32, (rows_mm, ent), 0)
        ohr[w] = (rows == row_of(2, w)).astype(BF16)
        picked = nn(src_t[...], ohs[w])
        both = nn(rel_t[...], ohr[w])
        scale = both[0:width] + both[width:]
        sr[w] = picked
        rr[w] = scale
        qt[w] = (picked * scale).astype(BF16)

    def finish(w, slot):
        block = part[slot]
        scores = nn(block, qt[w])
        rows = lax.broadcasted_iota(jnp.int32, (ent, ent), 0)
        hit = rows == row_of(1, w)
        chosen = (rows == row_of(3, w)).astype(F32)
        weight = jnp.sum(chosen, axis=1, keepdims=True) * (1.0 / ent)
        live = live_of(w)
        pos = jnp.sum(jnp.where(hit, scores, 0.0), axis=0, keepdims=True)
        dpos = -live * jax.nn.sigmoid(-pos)
        terms = jax.nn.sigmoid(scores) * weight * live
        pull = (terms + jnp.where(hit, dpos, 0.0)).astype(BF16)
        dquery = nn(block.T, pull)
        grown = nt(ohr[w], (dquery * sr[w]).astype(BF16))
        gr[0, 0:rows_mm, :] += grown[:, 0:half]
        gr[1, 0:rows_mm, :] += grown[:, half:]
        return pull, dquery

    def spread(w, pull, dquery):
        gw[w] = nt(pull, qt[w])
        return nt(ohs[w], (dquery * rr[w]).astype(BF16))

    prepare(0)
    pull, dquery = finish(0, 0)
    gs[...] = spread(0, pull, dquery)
    prepare(1)
    prepare(2)

    arrived(part.at[direct], part_recv.at[direct])
    forward = remote(
        part.at[direct], part.at[direct], fwd_send.at[0], part_recv.at[direct], sib
    )
    forward.start()

    @pl.when(core == 1)
    def _():
        arrived(part.at[3], part_recv.at[3])

    pull, dquery = finish(1, 2 + core)
    gs[...] += spread(1, pull, dquery)
    gb_send[...] = gw[1].astype(BF16)
    home_copy = remote(gb_send, gb_recv, g_send.at[0], g_recv.at[0], sib)

    @pl.when(core == 1)
    def _():
        home_copy.start()

    @pl.when(even)
    def _():
        for k in range(4):
            arrived(idx_far.at[k], far_recv.at[2 + k])
        arrived(ec_far, far_recv.at[1])
        arrived(src_far, far_recv.at[0])
        src_t[...] = src_far[...].T

    prepare(3)
    other = 1 + core
    arrived(part.at[other], part_recv.at[other])
    pull, dquery = finish(2, 1)
    gs[...] += spread(2, pull, dquery)
    pull, dquery = finish(3, 1 + core)

    swap = remote(
        gr.at[1 - core, pl.ds(0, rows_mm)], half_recv, h_send.at[0], h_recv.at[0], sib
    )
    swap.start()
    last = spread(3, pull, dquery)

    ga_send[...] = (gw[3] + jnp.where(even, gw[2], 0.0)).astype(BF16)
    pair_copy = remote(ga_send, ga_recv, g_send.at[1], g_recv.at[1], sib)
    pair_copy.start()
    gs_send[...] = last.astype(BF16)
    src_copy = remote(gs_send, gs_recv, g_send.at[2], g_recv.at[2], (grp, nxt))

    @pl.when(even)
    def _():
        src_copy.start()

    @pl.when(core == 1)
    def _():
        gs[...] += last

    arrived(half_recv, h_recv.at[0])
    if rows_mm < NX * xrows:
        xs[rows_mm:, :] = jnp.zeros((NX * xrows - rows_mm, half), BF16)
    xs[0:rows_mm, :] = (gr[core, 0:rows_mm, :] + half_recv[...]).astype(BF16)

    sent = [send_next, forward, swap, pair_copy]

    def rows_at(i, size):
        return pl.ds(pl.multiple_of(i * size, size), size)

    for k, i in enumerate(x_others):
        copy = remote(
            xs.at[rows_at(i, xrows)], x_recv.at[x], xs_send.at[k], xs_recv.at[x], at_x(i)
        )
        copy.start()
        sent.append(copy)

    arrived(ga_recv, g_recv.at[1])
    gh_send[...] = (gw[1 + core] + ga_recv[...].astype(F32)).astype(BF16)
    back = remote(gh_send, gh_recv, h_send.at[1], h_recv.at[1], (grp, prv))
    back.start()
    sent.append(back)

    total = xs[rows_at(x, xrows), :].astype(F32)
    for i in x_others:
        arrived(x_recv.at[i], xs_recv.at[i])
        total = total + x_recv[i].astype(F32)
    ys[...] = total.astype(BF16)
    for k, i in enumerate(y_others):
        copy = remote(
            ys.at[rows_at(i, chunk)], y_recv.at[y], ys_send.at[k], ys_recv.at[y], at_y(i)
        )
        copy.start()
        sent.append(copy)

    @pl.when(even)
    def _():
        arrived(gs_recv, g_recv.at[2])
        gs[...] += gs_recv[...].astype(F32)
        arrived(gb_recv, g_recv.at[0])
        gw[0] = gw[0] + gb_recv[...].astype(F32)

    gs_copy = pltpu.make_async_copy(gs, gs_out, out_sem.at[0])
    gs_copy.start()

    total = ys[rows_at(y, chunk), :].astype(F32)
    for i in y_others:
        arrived(y_recv.at[i], ys_recv.at[i])
        total = total + y_recv[i].astype(F32)
    z_all[z] = total
    for k, i in enumerate(z_others):
        copy = remote(z_all.at[z], z_all.at[z], zs_send.at[k], zs_recv.at[z], at_z(i))
        copy.start()
        sent.append(copy)

    arrived(gh_recv, h_recv.at[1])
    gw[0] = gw[0] + gh_recv[...].astype(F32)
    gd_copy = pltpu.make_async_copy(gw.at[0], gd_out, out_sem.at[1])
    gd_copy.start()

    for i in z_others:
        arrived(z_all.at[i], zs_recv.at[i])
    total = z_all[0]
    for i in range(1, nz):
        total = total + z_all[i]
    rel_all[core, x, y] = total.astype(BF16)
    for k, i in enumerate(y_others):
        piece = rel_all.at[core, x, y]
        copy = remote(piece, piece, ya_send.at[k], ya_recv.at[y], at_y(i))
        copy.start()
        sent.append(copy)
    for i in y_others:
        arrived(rel_all.at[core, x, i], ya_recv.at[i])
    for k, i in enumerate(x_others):
        piece = rel_all.at[core, x]
        copy = remote(piece, piece, xa_send.at[k], xa_recv.at[x], at_x(i))
        copy.start()
        sent.append(copy)
    for k, i in enumerate([x] + x_others):
        piece = rel_all.at[core, i]
        if k > 0:
            arrived(piece, xa_recv.at[i])
        copy = remote(piece, piece, ca_send.at[k], ca_recv.at[i], sib)
        copy.start()
        sent.append(copy)
    for i in range(NX):
        arrived(rel_all.at[1 - core, i], ca_recv.at[i])
    rel_copy = pltpu.make_async_copy(rel_all, rel_out, out_sem.at[2])
    rel_copy.start()

    for copy in sent:
        copy.wait_send()

    @pl.when(even)
    def _():
        send_sib.wait_send()
        for copy in far:
            copy.wait_send()
        src_copy.wait_send()

    @pl.when(core == 1)
    def _():
        home_copy.wait_send()

    gs_copy.wait()
    gd_copy.wait()
    rel_copy.wait()


def body(src_embed, dst_embed, relation, src_index, dst_index, rel_index, neg_index, edge_count):
    ent, width = src_embed.shape
    rels = relation.shape[0]
    steps = src_index.shape[2]
    nz = lax.axis_size("grp") // NX * ZLO
    half = width // 2
    chunk = -(-rels // (NX * NY * 16)) * 16
    rows_mm = -(-rels // 128) * 128
    xrows = NY * chunk
    tables = [t.reshape(steps, ent) for t in (src_index, dst_index, rel_index, neg_index)]
    vmem = pltpu.VMEM
    dma = pltpu.SemaphoreType.DMA
    scratch = [
        vmem((4, ent, width), BF16),
        vmem((ent, width), BF16),
        vmem((ent, width), BF16),
        vmem((rels, width), F32),
        vmem((rows_mm, width), F32),
        vmem((2 * width, rows_mm), BF16),
        vmem((width, ent), BF16),
        vmem((4, steps, ent), jnp.int32),
        vmem((4, steps, ent), jnp.int32),
        vmem((1, steps), jnp.int32),
        vmem((1, steps), jnp.int32),
        vmem((4, ent, ent), BF16),
        vmem((4, rows_mm, ent), BF16),
        vmem((4, width, ent), F32),
        vmem((4, width, ent), F32),
        vmem((4, width, ent), BF16),
        vmem((4, ent, width), F32),
        vmem((ent, width), F32),
        vmem((2, rows_mm, half), F32),
        vmem((ent, width), BF16),
        vmem((ent, width), BF16),
        vmem((ent, width), BF16),
        vmem((ent, width), BF16),
        vmem((ent, width), BF16),
        vmem((ent, width), BF16),
        vmem((ent, width), BF16),
        vmem((ent, width), BF16),
        vmem((rows_mm, half), F32),
        vmem((NX * xrows, half), BF16),
        vmem((NX, xrows, half), BF16),
        vmem((xrows, half), BF16),
        vmem((NY, chunk, half), BF16),
        vmem((nz, chunk, half), F32),
        vmem((2, NX, NY, chunk, half), BF16),
        dma((8,)),
        dma((3,)),
        dma((2,)),
        dma((4,)),
        dma((1,)),
        dma((6,)),
        dma((6,)),
        dma((3,)),
        dma((3,)),
        dma((2,)),
        dma((2,)),
        dma((NX,)), dma((NX,)),
        dma((NY,)), dma((NY,)),
        dma((nz,)), dma((nz,)),
        dma((NY,)), dma((NY,)),
        dma((NX,)), dma((NX,)),
        dma((NX,)), dma((NX,)),
    ]
    grad_src, grad_dst, rel_parts = pl.pallas_call(
        functools.partial(kernel, nz, rels, rows_mm, chunk),
        out_shape=(
            jax.ShapeDtypeStruct((ent, width), F32),
            jax.ShapeDtypeStruct((ent, width), F32),
            jax.ShapeDtypeStruct((2, NX, NY, chunk, half), BF16),
        ),
        in_specs=[pl.BlockSpec(memory_space=pl.ANY)] * 8,
        out_specs=(pl.BlockSpec(memory_space=pl.ANY),) * 3,
        scratch_shapes=scratch,
        compiler_params=pltpu.CompilerParams(
            collective_id=0, has_side_effects=True, vmem_limit_bytes=56 * 1024 * 1024
        ),
    )(src_embed, dst_embed, relation, *tables, edge_count.reshape(1, steps))
    rel_parts = rel_parts.reshape(2, NX * xrows, half)[:, :rels]
    grad_rel = jnp.concatenate([rel_parts[0], rel_parts[1]], axis=1).astype(F32)
    return (grad_src, grad_dst, grad_rel)


def solution(mesh):
    in_specs = (
        P(("grp", "blk"), None),
        P(("grp", "blk"), None),
        P(),
        P("grp", "blk", None, None),
        P("grp", "blk", None, None),
        P("grp", "blk", None, None),
        P("grp", "blk", None, None),
        P("grp", "blk", None),
    )
    out_specs = (P(("grp", "blk"), None), P(("grp", "blk"), None), P())
    return jax.shard_map(body, mesh=mesh, in_specs=in_specs, out_specs=out_specs, check_vma=False)
```

time: 401 us -> 68.7 us (0.17)
  waiting for transfers between devices: 265 us -> 0 us
  Pallas kernels: 0 us -> 64 us
  matrix products: 44.8 us -> 0 us
  other arithmetic: 29.6 us -> 1.18 us
  starting transfers between devices: 24.6 us -> 0 us
  local copies, waits for them, and re-layouts: 21.7 us -> 2.73 us
  between operations: 15 us -> 0.66 us
    psum x1 -> x0, waiting for transfers between devices: 251 us -> none  [body(): grad_rel = lax.psum(rel_total, ('grp', 'blk'))]
    pallas_call x0 -> x1, Pallas kernels: none -> 64 us  [body(): pl.pallas_call(functools.partial(kernel, nz, rels, rows_mm, chunk), out_s...]
    dot_general x36 -> x0, matrix products: 44.8 us -> none  [the longest x12 21.1 us: spread_rows(): lax.dot_general(table, values, (((0,), (0,)), ((), ())), precision=lax.Pr...]
    ppermute x7 -> x0, starting transfers between devices: 24.5 us -> none  [shifted(): return lax.ppermute(block, axis, route)]
    ppermute x7 -> x0, waiting for transfers between devices: 13.7 us -> none  [shifted(): return lax.ppermute(block, axis, route)]
    add x4 -> x0, other arithmetic: 13.1 us -> none  [the longest x2 9.88 us: body(): rel_total = rel_total + rel_part]
    scatter-add x2 -> x0, other arithmetic: 9.12 us -> none  [tile_terms(): grad_rel = jnp.zeros(relation.shape, jnp.float32).at[rel_rows_idx].add(dq...]
    gather x6 -> x0, local copies, waits for them, and re-layouts: 8.96 us -> none  [tile_terms(): rel_rows = jnp.take(relation, rel_rows_idx, axis=0)]
  transfers between devices with their start and end apart: 8 -> 0, of which waited for: 2 -> 0; matrix products, arithmetic and copies ran while one was open for 22% -> 0% of each run, Pallas kernels for 0% -> 0%
where the time goes in v1:
time: 68.7 us; the launch traced here: 68.6 us
  Pallas kernels  64 us (93%)
  local copies, waits for them, and re-layouts  2.73 us (4%)
  other arithmetic  1.18 us (2%)
    pallas_call x1, Pallas kernels, body(): pl.pallas_call(functools.partial(kernel, nz, rels, rows_mm, chunk), out_s...  64 us
    unnamed x6, local copies, waits for them, and re-layouts  1.59 us

profile of v1, /device:TPU:1, one launch (start us, length us, event | category | flops | bytes accessed | tf_op | source)
XLA Modules:
  0.0 68.6 jit_solution(17296760656311721397)
XLA Ops:
  0.6 64.0 %shard_map.103 = (f32[512,256]{1,0:T(8,128)}, f32[512,256]{1,0:T(8,128)}, bf16[2,4,8,48,128]{4,3,2,1,0:T(8,128)(2,1)}) custom-call(bf16[512,256]{1,0:T(8,128)(2,1)} %src_hbm.1, bf16[512,256]{1,0:T(8,128)(2,1)} %dst_hbm.1, f32[1345,256]{1,0:T(8,128)} %rel_hbm.1, s32[4,512]{1,0:T(4,128)} %bitcast.11, s32[4,512]{1,0:T(4,128)} %bitcast.12, s32[4,512]{1,0:T(4,128)} %bitcast.13, ...), custom_call_target="tpu_custom_call" | custom-call | tf_op jit(solution)/shard_map/pallas_call | solution.py:411
  64.7 1.1 %slice_bitcast_fusion.1 = (bf16[1345,128]{1,0:T(8,128)(2,1)S(1)}, bf16[1345,128]{1,0:T(8,128)(2,1)S(1)}) fusion(bf16[2,1536,128]{2,1,0:T(8,128)(2,1)} %bitcast.10), kind=kLoop, calls=%fused_computation.2 | loop fusion | bytes 1377280 | tf_op jit(solution)/shard_map/squeeze | solution.py:426
  65.8 0.0 copy-start.1
  65.8 0.0 copy-start
  65.8 1.2 %maximum_convert_fusion = f32[1345,256]{1,0:T(8,128)} fusion(bf16[1345,128]{1,0:T(8,128)(2,1)S(1)} %get-tuple-element.10, bf16[1345,128]{1,0:T(8,128)(2,1)S(1)} %get-tuple-element.9), kind=kLoop, calls=%fused_computation | loop fusion | flops 1377280 | bytes 2065920 | tf_op jit(solution)/shard_map/convert_element_type | solution.py:426
  67.0 0.0 copy-done.1
  67.0 0.8 %copy.13 = f32[512,256]{1,0:T(8,128)} copy(f32[512,256]{1,0:T(8,128)S(1)} %copy-done.1) | data formatting | bytes 1048576
  67.8 0.0 copy-done
  67.8 0.8 %copy.14 = f32[512,256]{1,0:T(8,128)} copy(f32[512,256]{1,0:T(8,128)S(1)} %copy-done) | data formatting | bytes 1048576
Async XLA Ops:
  65.8 1.2 %copy-start.1 = (f32[512,256]{1,0:T(8,128)S(1)}, f32[512,256]{1,0:T(8,128)}, u32[]{:S(2)}) copy-start(f32[512,256]{1,0:T(8,128)} %get-tuple-element.14) | copy-start | bytes 1572868
  65.8 2.0 %copy-start = (f32[512,256]{1,0:T(8,128)S(1)}, f32[512,256]{1,0:T(8,128)}, u32[]{:S(2)}) copy-start(f32[512,256]{1,0:T(8,128)} %get-tuple-element.15) | copy-start | bytes 1572868

commit v2 on v1

v2 whole, which is shorter than its diff:
```python
import functools

import jax
import jax.numpy as jnp
from jax import lax
from jax.experimental import pallas as pl
from jax.experimental.pallas import tpu as pltpu
from jax.sharding import PartitionSpec as P

MESH = pl.DeviceIdType.MESH
F32 = jnp.float32
BF16 = jnp.bfloat16
NX = 4
NY = 8
ZLO = 2
CHUNK = 16


def nt(a, b):
    return lax.dot_general(a, b, (((1,), (1,)), ((), ())), preferred_element_type=F32)


def nn(a, b):
    return jnp.dot(a, b, preferred_element_type=F32)


def kernel(
    nz, rels, rows_mm, pieces,
    src_hbm, dst_hbm, rel_hbm, si_hbm, di_hbm, ri_hbm, ni_hbm, ec_hbm,
    gs_out, gd_out, rel_out,
    part, src_v, src_far, rel_v, rel_pad, rel_t, src_t, idx, idx_far, ec, ec_far,
    ohs, ohr, sr, rr, qt, weight, pulls, back_v, gw, gs, gr,
    gs_send, gs_recv, ga_send, ga_recv, gb_send, gb_recv, gh_send, gh_recv,
    half_recv, xs, x_recv, ys, y_recv, z_all, rel_all,
    in_sem, out_sem, part_send, part_recv, fwd_send, far_send, far_recv,
    g_send, g_recv, h_send, h_recv, s_send, s_recv,
    xs_send, xs_recv, ys_send, ys_recv, zs_send, zs_recv,
    ya_send, ya_recv, xa_send, xa_recv, ca_send, ca_recv,
):
    ent, width = dst_hbm.shape
    half = width // 2
    yrows = CHUNK
    xrows = NY * yrows
    prows = NX * xrows
    nchip = ZLO * NY
    grp, blk = lax.axis_index("grp"), lax.axis_index("blk")
    core = lax.rem(blk, 2)
    chip = blk // 2
    y = lax.rem(chip, NY)
    z = (grp // NX) * ZLO + chip // NY
    x = lax.rem(grp, NX)
    even = core == 0
    nxt = lax.rem(chip + 1, nchip) * 2 + core
    prv = lax.rem(chip + nchip - 1, nchip) * 2 + core
    sib = (grp, chip * 2 + 1 - core)

    def at_x(i):
        return ((grp // NX) * NX + i, blk)

    def at_y(i):
        return (grp, (chip // NY) * NY * 2 + i * 2 + core)

    def at_z(i):
        return ((i // ZLO) * NX + x, lax.rem(i, ZLO) * NY * 2 + y * 2 + core)

    x_others = [lax.rem(x + k, NX) for k in range(1, NX)]
    y_others = [lax.rem(y + k, NY) for k in range(1, NY)]
    z_others = [lax.rem(z + k, nz) for k in range(1, nz)]

    def remote(source, target, send, recv, device):
        return pltpu.make_async_remote_copy(
            src_ref=source, dst_ref=target, send_sem=send, recv_sem=recv,
            device_id=device, device_id_type=MESH,
        )

    def arrived(target, recv):
        remote(target, target, recv, recv, sib).wait_recv()

    barrier = pltpu.get_barrier_semaphore()
    greet = [sib, (grp, nxt), (grp, prv)]
    greet += [at_x(i) for i in x_others] + [at_y(i) for i in y_others] + [at_z(i) for i in z_others]
    for device in greet:
        pl.semaphore_signal(barrier, inc=1, device_id=device, device_id_type=MESH)

    own = [(si_hbm, 0), (di_hbm, 1), (ri_hbm, 2), (ni_hbm, 3)]
    loads = [
        pltpu.make_async_copy(rel_hbm, rel_v, in_sem.at[0]),
        pltpu.make_async_copy(src_hbm, src_v, in_sem.at[1]),
        pltpu.make_async_copy(dst_hbm, part.at[0], in_sem.at[2]),
        pltpu.make_async_copy(ec_hbm, ec, in_sem.at[3]),
    ] + [pltpu.make_async_copy(ref, idx.at[k], in_sem.at[4 + k]) for ref, k in own]
    for load in loads:
        load.start()
    if rows_mm < pieces * prows:
        gr[:, rows_mm:, :] = jnp.zeros((2, pieces * prows - rows_mm, half), F32)
    tail = rels // 8 * 8
    rel_pad[tail:, :] = jnp.zeros((rows_mm - tail, width), F32)
    for load in loads:
        load.wait()
    rel_pad[0:rels, :] = rel_v[...]
    rel_t[...] = rel_pad[...].astype(BF16).T
    src_t[...] = src_v[...].T

    pl.semaphore_wait(barrier, len(greet))

    direct = 2 - core
    send_next = remote(
        dst_hbm, part.at[direct], part_send.at[0], part_recv.at[direct], (grp, nxt)
    )
    send_next.start()
    send_sib = remote(dst_hbm, part.at[3], part_send.at[1], part_recv.at[3], sib)
    far = [remote(src_hbm, src_far, far_send.at[0], far_recv.at[0], (grp, prv))]
    far += [remote(ec_hbm, ec_far, far_send.at[1], far_recv.at[1], (grp, prv))]
    far += [
        remote(ref, idx_far.at[k], far_send.at[2 + k], far_recv.at[2 + k], (grp, prv))
        for ref, k in own
    ]

    @pl.when(even)
    def _():
        send_sib.start()
        for copy in far:
            copy.start()

    def tile_of(w):
        if w in (0, 3):
            return w
        return jnp.where(even, 3 - w, w)

    def row_of(k, w):
        row = idx[k, pl.ds(tile_of(w), 1), :]
        if w == 3:
            row = jnp.where(even, idx_far[k, 3:4, :], row)
        return row

    def live_of(w):
        counts = ec[...].astype(F32)
        if w == 3:
            counts = jnp.where(even, ec_far[...].astype(F32), counts)
        place = lax.broadcasted_iota(jnp.int32, counts.shape, 1)
        count = jnp.sum(jnp.where(place == tile_of(w), counts, 0.0), axis=1, keepdims=True)
        slot = lax.broadcasted_iota(jnp.int32, (1, ent), 1).astype(F32)
        return slot < count

    def prepare(w):
        rows = lax.broadcasted_iota(jnp.int32, (ent, ent), 0)
        ohs[w] = (rows == jnp.where(live_of(w), row_of(0, w), -1)).astype(BF16)
        chosen = (rows == row_of(3, w)).astype(F32)
        weight[w] = jnp.sum(chosen, axis=1, keepdims=True) * (1.0 / ent)
        rows = lax.broadcasted_iota(jnp.int32, (rows_mm, ent), 0)
        ohr[w] = (rows == row_of(2, w)).astype(BF16)
        picked = nn(src_t[...], ohs[w])
        scale = nn(rel_t[...], ohr[w])
        sr[w] = picked.astype(BF16)
        rr[w] = scale.astype(BF16)
        qt[w] = (picked * scale).astype(BF16)

    def finish(w, slot):
        block = part[slot]
        scores = nn(block, qt[w])
        rows = lax.broadcasted_iota(jnp.int32, (ent, ent), 0)
        hit = rows == row_of(1, w)
        pos = jnp.sum(jnp.where(hit, scores, 0.0), axis=0, keepdims=True)
        dpos = -jax.nn.sigmoid(-pos)
        terms = pl.reciprocal(1.0 + jnp.exp(-scores), approx=True) * weight[w]
        pull = (terms + jnp.where(hit, dpos, 0.0)).astype(BF16)
        pulls[w] = pull
        dquery = nn(block.T, pull)
        back_v[w] = (dquery * rr[w].astype(F32)).astype(BF16)
        value = (dquery * sr[w].astype(F32)).astype(BF16)
        for p in range(pieces):
            low, high = p * prows, min((p + 1) * prows, rows_mm)
            grown = nt(ohr[w, low:high, :], value)
            for h in range(2):
                grown_half = grown[:, h * half:(h + 1) * half]
                if w == 0:
                    gr[h, low:high, :] = grown_half
                else:
                    gr[h, low:high, :] += grown_half
            if w == 3:
                swaps[p].start()

    def spread(w):
        gw[w] = nt(pulls[w], qt[w])
        return nt(ohs[w], back_v[w])

    swaps = [
        remote(
            gr.at[1 - core, pl.ds(p * prows, prows)], half_recv.at[p],
            s_send.at[p], s_recv.at[p], sib,
        )
        for p in range(pieces)
    ]

    prepare(0)
    finish(0, 0)
    prepare(1)
    prepare(2)

    arrived(part.at[direct], part_recv.at[direct])
    forward = remote(
        part.at[direct], part.at[direct], fwd_send.at[0], part_recv.at[direct], sib
    )
    forward.start()

    @pl.when(even)
    def _():
        for k in range(4):
            arrived(idx_far.at[k], far_recv.at[2 + k])
        arrived(ec_far, far_recv.at[1])
        arrived(src_far, far_recv.at[0])
        src_t[...] = src_far[...].T

    @pl.when(core == 1)
    def _():
        arrived(part.at[3], part_recv.at[3])

    prepare(3)
    finish(1, 2 + core)
    other = 1 + core
    arrived(part.at[other], part_recv.at[other])
    finish(2, 1)
    finish(3, 1 + core)

    sent = [send_next, forward] + swaps

    def rows_at(i, size):
        return pl.ds(pl.multiple_of(i * size, size), size)

    gs[...] = spread(0) + spread(1)
    for p in range(pieces):
        arrived(half_recv.at[p], s_recv.at[p])
        xs[p] = (gr[core, p * prows:(p + 1) * prows, :] + half_recv[p]).astype(BF16)
        for k, i in enumerate(x_others):
            copy = remote(
                xs.at[p, rows_at(i, xrows)], x_recv.at[p, x],
                xs_send.at[p, k], xs_recv.at[p, x], at_x(i),
            )
            copy.start()
            sent.append(copy)

    gs[...] += spread(2)
    last = spread(3)
    gb_send[...] = gw[1].astype(BF16)
    home_copy = remote(gb_send, gb_recv, g_send.at[0], g_recv.at[0], sib)
    ga_send[...] = (gw[3] + jnp.where(even, gw[2], 0.0)).astype(BF16)
    pair_copy = remote(ga_send, ga_recv, g_send.at[1], g_recv.at[1], sib)
    pair_copy.start()
    sent.append(pair_copy)
    gs_send[...] = last.astype(BF16)
    src_copy = remote(gs_send, gs_recv, g_send.at[2], g_recv.at[2], (grp, nxt))

    @pl.when(even)
    def _():
        src_copy.start()

    @pl.when(core == 1)
    def _():
        home_copy.start()
        gs[...] += last

    for p in range(pieces):
        total = xs[p, rows_at(x, xrows), :].astype(F32)
        for i in x_others:
            arrived(x_recv.at[p, i], xs_recv.at[p, i])
            total = total + x_recv[p, i].astype(F32)
        ys[p] = total.astype(BF16)
        for k, i in enumerate(y_others):
            copy = remote(
                ys.at[p, rows_at(i, yrows)], y_recv.at[p, y],
                ys_send.at[p, k], ys_recv.at[p, y], at_y(i),
            )
            copy.start()
            sent.append(copy)

    arrived(ga_recv, g_recv.at[1])
    gh_send[...] = (gw[1 + core] + ga_recv[...].astype(F32)).astype(BF16)
    homeward = remote(gh_send, gh_recv, h_send.at[0], h_recv.at[0], (grp, prv))
    homeward.start()
    sent.append(homeward)

    for p in range(pieces):
        total = ys[p, rows_at(y, yrows), :].astype(F32)
        for i in y_others:
            arrived(y_recv.at[p, i], ys_recv.at[p, i])
            total = total + y_recv[p, i].astype(F32)
        z_all[p, z] = total
        for k, i in enumerate(z_others):
            copy = remote(
                z_all.at[p, z], z_all.at[p, z], zs_send.at[p, k], zs_recv.at[p, z], at_z(i)
            )
            copy.start()
            sent.append(copy)

    @pl.when(even)
    def _():
        arrived(gs_recv, g_recv.at[2])
        gs[...] += gs_recv[...].astype(F32)
        arrived(gb_recv, g_recv.at[0])
        gw[0] = gw[0] + gb_recv[...].astype(F32)

    gs_copy = pltpu.make_async_copy(gs, gs_out, out_sem.at[0])
    gs_copy.start()

    for p in range(pieces):
        for i in z_others:
            arrived(z_all.at[p, i], zs_recv.at[p, i])
        total = z_all[p, 0]
        for i in range(1, nz):
            total = total + z_all[p, i]
        piece = rel_all.at[core, p, x, y]
        piece[...] = total.astype(BF16)
        for k, i in enumerate(y_others):
            copy = remote(piece, piece, ya_send.at[p, k], ya_recv.at[p, y], at_y(i))
            copy.start()
            sent.append(copy)

    arrived(gh_recv, h_recv.at[0])
    gw[0] = gw[0] + gh_recv[...].astype(F32)
    gd_copy = pltpu.make_async_copy(gw.at[0], gd_out, out_sem.at[1])
    gd_copy.start()

    for p in range(pieces):
        for i in y_others:
            arrived(rel_all.at[core, p, x, i], ya_recv.at[p, i])
        piece = rel_all.at[core, p, x]
        for k, i in enumerate(x_others):
            copy = remote(piece, piece, xa_send.at[p, k], xa_recv.at[p, x], at_x(i))
            copy.start()
            sent.append(copy)
    for p in range(pieces):
        for i in x_others:
            arrived(rel_all.at[core, p, i], xa_recv.at[p, i])
        piece = rel_all.at[core, p]
        copy = remote(piece, piece, ca_send.at[p], ca_recv.at[p], sib)
        copy.start()
        sent.append(copy)
    rel_copies = []
    for p in range(pieces):
        arrived(rel_all.at[1 - core, p], ca_recv.at[p])
        for h in range(2):
            copy = pltpu.make_async_copy(
                rel_all.at[h, p], rel_out.at[h, p], out_sem.at[2 + 2 * p + h]
            )
            copy.start()
            rel_copies.append(copy)

    for copy in sent:
        copy.wait_send()

    @pl.when(even)
    def _():
        send_sib.wait_send()
        for copy in far:
            copy.wait_send()
        src_copy.wait_send()

    @pl.when(core == 1)
    def _():
        home_copy.wait_send()

    gs_copy.wait()
    gd_copy.wait()
    for copy in rel_copies:
        copy.wait()


def store_kernel(
    rels, gs_in, gd_in, rel_in, gs_out, gd_out, rel_out, rel_b, rel_f, gs_v, gd_v, in_sem, out_sem
):
    ins = [
        pltpu.make_async_copy(rel_in, rel_b, in_sem.at[0]),
        pltpu.make_async_copy(gs_in, gs_v, in_sem.at[1]),
        pltpu.make_async_copy(gd_in, gd_v, in_sem.at[2]),
    ]
    outs = [
        pltpu.make_async_copy(rel_f, rel_out, out_sem.at[0]),
        pltpu.make_async_copy(gs_v, gs_out, out_sem.at[1]),
        pltpu.make_async_copy(gd_v, gd_out, out_sem.at[2]),
    ]
    for copy in ins:
        copy.start()
    half = rel_b.shape[2]
    ins[0].wait()
    for h in range(2):
        rel_f[:, h * half:(h + 1) * half] = rel_b[h, 0:rels, :].astype(F32)
    outs[0].start()
    for k in (1, 2):
        ins[k].wait()
        outs[k].start()
    for copy in outs:
        copy.wait()


def body(src_embed, dst_embed, relation, src_index, dst_index, rel_index, neg_index, edge_count):
    ent, width = src_embed.shape
    rels = relation.shape[0]
    steps = src_index.shape[2]
    nz = lax.axis_size("grp") // NX * ZLO
    half = width // 2
    pieces = -(-rels // (NX * NY * CHUNK))
    rows_mm = -(-rels // 128) * 128
    xrows = NY * CHUNK
    prows = NX * xrows
    tables = [t.reshape(steps, ent) for t in (src_index, dst_index, rel_index, neg_index)]
    vmem = pltpu.VMEM
    dma = pltpu.SemaphoreType.DMA
    block = vmem((ent, width), BF16)
    scratch = [
        vmem((4, ent, width), BF16),
        block,
        block,
        vmem((rels, width), F32),
        vmem((rows_mm, width), F32),
        vmem((width, rows_mm), BF16),
        vmem((width, ent), BF16),
        vmem((4, steps, ent), jnp.int32),
        vmem((4, steps, ent), jnp.int32),
        vmem((1, steps), jnp.int32),
        vmem((1, steps), jnp.int32),
        vmem((4, ent, ent), BF16),
        vmem((4, rows_mm, ent), BF16),
        vmem((4, width, ent), BF16),
        vmem((4, width, ent), BF16),
        vmem((4, width, ent), BF16),
        vmem((4, ent, 1), F32),
        vmem((4, ent, ent), BF16),
        vmem((4, width, ent), BF16),
        vmem((4, ent, width), F32),
        vmem((ent, width), F32),
        vmem((2, pieces * prows, half), F32),
        block, block, block, block, block, block, block, block,
        vmem((pieces, prows, half), F32),
        vmem((pieces, prows, half), BF16),
        vmem((pieces, NX, xrows, half), BF16),
        vmem((pieces, xrows, half), BF16),
        vmem((pieces, NY, CHUNK, half), BF16),
        vmem((pieces, nz, CHUNK, half), F32),
        vmem((2, pieces, NX, NY, CHUNK, half), BF16),
        dma((8,)),
        dma((2 + 2 * pieces,)),
        dma((2,)),
        dma((4,)),
        dma((1,)),
        dma((6,)),
        dma((6,)),
        dma((3,)),
        dma((3,)),
        dma((1,)),
        dma((1,)),
        dma((pieces,)), dma((pieces,)),
        dma((pieces, NX)), dma((pieces, NX)),
        dma((pieces, NY)), dma((pieces, NY)),
        dma((pieces, nz)), dma((pieces, nz)),
        dma((pieces, NY)), dma((pieces, NY)),
        dma((pieces, NX)), dma((pieces, NX)),
        dma((pieces,)), dma((pieces,)),
    ]
    anywhere = pl.BlockSpec(memory_space=pl.ANY)
    grad = jax.ShapeDtypeStruct((ent, width), F32)
    grad_src, grad_dst, rel_parts = pl.pallas_call(
        functools.partial(kernel, nz, rels, rows_mm, pieces),
        out_shape=(
            grad, grad, jax.ShapeDtypeStruct((2, pieces, NX, NY, CHUNK, half), BF16)
        ),
        in_specs=[anywhere] * 8,
        out_specs=(anywhere,) * 3,
        scratch_shapes=scratch,
        compiler_params=pltpu.CompilerParams(
            collective_id=0, has_side_effects=True, vmem_limit_bytes=56 * 1024 * 1024
        ),
    )(src_embed, dst_embed, relation, *tables, edge_count.reshape(1, steps))
    rel_parts = rel_parts.reshape(2, pieces * prows, half)
    return pl.pallas_call(
        functools.partial(store_kernel, rels),
        out_shape=(grad, grad, jax.ShapeDtypeStruct((rels, width), F32)),
        in_specs=[anywhere] * 3,
        out_specs=(anywhere,) * 3,
        scratch_shapes=[
            vmem(rel_parts.shape, BF16), vmem((rels, width), F32),
            vmem((ent, width), F32), vmem((ent, width), F32), dma((3,)), dma((3,)),
        ],
        compiler_params=pltpu.CompilerParams(vmem_limit_bytes=16 * 1024 * 1024),
    )(grad_src, grad_dst, rel_parts)


def solution(mesh):
    in_specs = (
        P(("grp", "blk"), None),
        P(("grp", "blk"), None),
        P(),
        P("grp", "blk", None, None),
        P("grp", "blk", None, None),
        P("grp", "blk", None, None),
        P("grp", "blk", None, None),
        P("grp", "blk", None),
    )
    out_specs = (P(("grp", "blk"), None), P(("grp", "blk"), None), P())
    return jax.shard_map(body, mesh=mesh, in_specs=in_specs, out_specs=out_specs, check_vma=False)
```

time: 68.7 us -> 67.1 us (0.977)
  other arithmetic: 1.18 us -> 0 us
  Pallas kernels: 64 us -> 62.9 us
    unnamed x6, local copies, waits for them, and re-layouts: 1.59 us -> 3.21 us
    convert_element_type x1 -> x0, other arithmetic: 1.18 us -> none  [body(): grad_rel = jnp.concatenate([rel_parts[0], rel_parts[1]], axis=1).astype(F32)]
    squeeze x1 -> x0, local copies, waits for them, and re-layouts: 1.13 us -> none  [body(): grad_rel = jnp.concatenate([rel_parts[0], rel_parts[1]], axis=1).astype(F32)]
    pallas_call x1 -> x2, Pallas kernels: 64 us -> 62.9 us  [the longest x1 61.2 us: body(): pl.pallas_call(functools.partial(kernel, nz, rels, rows_mm, pieces), out_...]
where the time goes in v2:
time: 67.1 us; the launch traced here: 66.8 us
  Pallas kernels  62.9 us (94%)
  local copies, waits for them, and re-layouts  3.21 us (5%)
    pallas_call x1, Pallas kernels, body(): pl.pallas_call(functools.partial(kernel, nz, rels, rows_mm, pieces), out_...  61.2 us
    unnamed x6, local copies, waits for them, and re-layouts  3.21 us
    pallas_call x1, Pallas kernels, body(): pl.pallas_call(functools.partial(store_kernel, rels), out_shape=(grad, gr...  1.69 us

profile of v2, /device:TPU:1, one launch (start us, length us, event | category | flops | bytes accessed | tf_op | source)
XLA Modules:
  0.0 66.8 jit_solution(15310507024595526754)
XLA Ops:
  0.6 61.2 %shard_map.103 = (f32[512,256]{1,0:T(8,128)}, f32[512,256]{1,0:T(8,128)}, bf16[2,3,4,8,16,128]{5,4,3,2,1,0:T(8,128)(2,1)}) custom-call(bf16[512,256]{1,0:T(8,128)(2,1)} %src_hbm.1, bf16[512,256]{1,0:T(8,128)(2,1)} %dst_hbm.1, f32[1345,256]{1,0:T(8,128)} %rel_hbm.1, s32[4,512]{1,0:T(4,128)} %bitcast.7, s32[4,512]{1,0:T(4,128)} %bitcast.8, s32[4,512]{1,0:T(4,128)} %bitcast.9, ...), custom_call_target="tpu_custom_call" | custom-call | tf_op jit(solution)/shard_map/pallas_call | solution.py:461
  61.9 0.0 copy-start
  61.9 1.1 %copy-done = bf16[2,3,4,8,16,128]{5,4,3,2,1,0:T(8,128)(2,1)S(1)} copy-done((bf16[2,3,4,8,16,128]{5,4,3,2,1,0:T(8,128)(2,1)S(1)}, bf16[2,3,4,8,16,128]{5,4,3,2,1,0:T(8,128)(2,1)}, u32[]{:S(2)}) %copy-start) | copy-done | bytes 786456
  63.0 0.0 copy-start.1
  63.0 1.0 %copy-done.1 = f32[512,256]{1,0:T(8,128)S(1)} copy-done((f32[512,256]{1,0:T(8,128)S(1)}, f32[512,256]{1,0:T(8,128)}, u32[]{:S(2)}) %copy-start.1) | copy-done | bytes 524312
  64.1 0.0 copy-start.2
  64.1 1.0 %copy-done.2 = f32[512,256]{1,0:T(8,128)S(1)} copy-done((f32[512,256]{1,0:T(8,128)S(1)}, f32[512,256]{1,0:T(8,128)}, u32[]{:S(2)}) %copy-start.2) | copy-done | bytes 524312
  65.1 1.7 %shard_map.104 = (f32[512,256]{1,0:T(8,128)}, f32[512,256]{1,0:T(8,128)}, f32[1345,256]{1,0:T(8,128)}) custom-call(f32[512,256]{1,0:T(8,128)S(1)} %copy-done.1, f32[512,256]{1,0:T(8,128)S(1)} %copy-done.2, bf16[2,1536,128]{2,1,0:T(8,128)(2,1)S(1)} %bitcast.6), custom_call_target="tpu_custom_call" | custom-call | tf_op jit(solution)/shard_map/pallas_call | solution.py:474
Async XLA Ops:
  61.9 1.1 %copy-start = (bf16[2,3,4,8,16,128]{5,4,3,2,1,0:T(8,128)(2,1)S(1)}, bf16[2,3,4,8,16,128]{5,4,3,2,1,0:T(8,128)(2,1)}, u32[]{:S(2)}) copy-start(bf16[2,3,4,8,16,128]{5,4,3,2,1,0:T(8,128)(2,1)} %get-tuple-element.8) | copy-start | bytes 2359300
  63.0 1.0 %copy-start.1 = (f32[512,256]{1,0:T(8,128)S(1)}, f32[512,256]{1,0:T(8,128)}, u32[]{:S(2)}) copy-start(f32[512,256]{1,0:T(8,128)} %get-tuple-element.6.gs_in) | copy-start | bytes 1572868
  64.1 1.0 %copy-start.2 = (f32[512,256]{1,0:T(8,128)S(1)}, f32[512,256]{1,0:T(8,128)}, u32[]{:S(2)}) copy-start(f32[512,256]{1,0:T(8,128)} %get-tuple-element.7.gd_in) | copy-start | bytes 1572868

commit v3 on v2

--- a/solution.py
+++ b/solution.py
@@ -14,6 +14,7 @@
 NY = 8
 ZLO = 2
 CHUNK = 16
+STEP = 128
 
 
 def nt(a, b):
@@ -31,9 +32,9 @@
     part, src_v, src_far, rel_v, rel_pad, rel_t, src_t, idx, idx_far, ec, ec_far,
     ohs, ohr, sr, rr, qt, weight, pulls, back_v, gw, gs, gr,
     gs_send, gs_recv, ga_send, ga_recv, gb_send, gb_recv, gh_send, gh_recv,
-    half_recv, xs, x_recv, ys, y_recv, z_all, rel_all,
-    in_sem, out_sem, part_send, part_recv, fwd_send, far_send, far_recv,
-    g_send, g_recv, h_send, h_recv, s_send, s_recv,
+    half_recv, xs, x_recv, ys, y_recv, z_all, rel_own,
+    in_sem, out_sem, part_send, part_recv, far_send, far_recv,
+    g_send, g_recv, s_send, s_recv,
     xs_send, xs_recv, ys_send, ys_recv, zs_send, zs_recv,
     ya_send, ya_recv, xa_send, xa_recv, ca_send, ca_recv,
 ):
@@ -73,8 +74,8 @@
             device_id=device, device_id_type=MESH,
         )
 
-    def arrived(target, recv):
-        remote(target, target, recv, recv, sib).wait_recv()
+    def arrived(buffer, recv):
+        pltpu.make_async_copy(buffer, buffer, recv).wait()
 
     barrier = pltpu.get_barrier_semaphore()
     greet = [sib, (grp, nxt), (grp, prv)]
@@ -88,8 +89,8 @@
         pltpu.make_async_copy(src_hbm, src_v, in_sem.at[1]),
         pltpu.make_async_copy(dst_hbm, part.at[0], in_sem.at[2]),
         pltpu.make_async_copy(ec_hbm, ec, in_sem.at[3]),
-    ] + [pltpu.make_async_copy(ref, idx.at[k], in_sem.at[4 + k]) for ref, k in own]
-    for load in loads:
+    ]
+    for load in loads + [pltpu.make_async_copy(ref, idx.at[k], in_sem.at[4]) for ref, k in own]:
         load.start()
     if rows_mm < pieces * prows:
         gr[:, rows_mm:, :] = jnp.zeros((2, pieces * prows - rows_mm, half), F32)
@@ -97,8 +98,12 @@
     rel_pad[tail:, :] = jnp.zeros((rows_mm - tail, width), F32)
     for load in loads:
         load.wait()
+    arrived(idx, in_sem.at[4])
     rel_pad[0:rels, :] = rel_v[...]
-    rel_t[...] = rel_pad[...].astype(BF16).T
+    turned = rel_pad[...].T
+    high = turned.astype(BF16)
+    rel_t[0:width, :] = high
+    rel_t[width:, :] = (turned - high.astype(F32)).astype(BF16)
     src_t[...] = src_v[...].T
 
     pl.semaphore_wait(barrier, len(greet))
@@ -112,7 +117,7 @@
     far = [remote(src_hbm, src_far, far_send.at[0], far_recv.at[0], (grp, prv))]
     far += [remote(ec_hbm, ec_far, far_send.at[1], far_recv.at[1], (grp, prv))]
     far += [
-        remote(ref, idx_far.at[k], far_send.at[2 + k], far_recv.at[2 + k], (grp, prv))
+        remote(ref, idx_far.at[k], far_send.at[2], far_recv.at[2], (grp, prv))
         for ref, k in own
     ]
 
@@ -150,23 +155,24 @@
         rows = lax.broadcasted_iota(jnp.int32, (rows_mm, ent), 0)
         ohr[w] = (rows == row_of(2, w)).astype(BF16)
         picked = nn(src_t[...], ohs[w])
-        scale = nn(rel_t[...], ohr[w])
+        both = nn(rel_t[...], ohr[w])
+        scale = both[0:width] + both[width:]
         sr[w] = picked.astype(BF16)
-        rr[w] = scale.astype(BF16)
+        rr[w] = scale
         qt[w] = (picked * scale).astype(BF16)
 
     def finish(w, slot):
         block = part[slot]
-        scores = nn(block, qt[w])
-        rows = lax.broadcasted_iota(jnp.int32, (ent, ent), 0)
-        hit = rows == row_of(1, w)
-        pos = jnp.sum(jnp.where(hit, scores, 0.0), axis=0, keepdims=True)
-        dpos = -jax.nn.sigmoid(-pos)
-        terms = pl.reciprocal(1.0 + jnp.exp(-scores), approx=True) * weight[w]
-        pull = (terms + jnp.where(hit, dpos, 0.0)).astype(BF16)
-        pulls[w] = pull
+        for low in range(0, ent, STEP):
+            scores = nn(block[low:low + STEP], qt[w])
+            rows = low + lax.broadcasted_iota(jnp.int32, (STEP, ent), 0)
+            decay = jnp.exp(jnp.minimum(-scores, 87.0))
+            share = weight[w, low:low + STEP]
+            share = jnp.where(rows == row_of(1, w), share - decay, share)
+            pulls[w, low:low + STEP] = (pl.reciprocal(1.0 + decay, approx=True) * share).astype(BF16)
+        pull = pulls[w]
         dquery = nn(block.T, pull)
-        back_v[w] = (dquery * rr[w].astype(F32)).astype(BF16)
+        back_v[w] = (dquery * rr[w]).astype(BF16)
         value = (dquery * sr[w].astype(F32)).astype(BF16)
         for p in range(pieces):
             low, high = p * prows, min((p + 1) * prows, rows_mm)
@@ -199,14 +205,13 @@
 
     arrived(part.at[direct], part_recv.at[direct])
     forward = remote(
-        part.at[direct], part.at[direct], fwd_send.at[0], part_recv.at[direct], sib
+        part.at[direct], part.at[direct], part_send.at[2], part_recv.at[direct], sib
     )
     forward.start()
 
     @pl.when(even)
     def _():
-        for k in range(4):
-            arrived(idx_far.at[k], far_recv.at[2 + k])
+        arrived(idx_far, far_recv.at[2])
         arrived(ec_far, far_recv.at[1])
         arrived(src_far, far_recv.at[0])
         src_t[...] = src_far[...].T
@@ -232,23 +237,19 @@
         arrived(half_recv.at[p], s_recv.at[p])
         xs[p] = (gr[core, p * prows:(p + 1) * prows, :] + half_recv[p]).astype(BF16)
         for k, i in enumerate(x_others):
-            copy = remote(
-                xs.at[p, rows_at(i, xrows)], x_recv.at[p, x],
-                xs_send.at[p, k], xs_recv.at[p, x], at_x(i),
-            )
-            copy.start()
-            sent.append(copy)
+            remote(
+                xs.at[p, rows_at(i, xrows)], x_recv.at[p, k], xs_send.at[p], xs_recv.at[p], at_x(i)
+            ).start()
 
     gs[...] += spread(2)
     last = spread(3)
-    gb_send[...] = gw[1].astype(BF16)
-    home_copy = remote(gb_send, gb_recv, g_send.at[0], g_recv.at[0], sib)
     ga_send[...] = (gw[3] + jnp.where(even, gw[2], 0.0)).astype(BF16)
     pair_copy = remote(ga_send, ga_recv, g_send.at[1], g_recv.at[1], sib)
     pair_copy.start()
-    sent.append(pair_copy)
     gs_send[...] = last.astype(BF16)
     src_copy = remote(gs_send, gs_recv, g_send.at[2], g_recv.at[2], (grp, nxt))
+    gb_send[...] = gw[1].astype(BF16)
+    home_copy = remote(gb_send, gb_recv, g_send.at[0], g_recv.at[0], sib)
 
     @pl.when(even)
     def _():
@@ -259,91 +260,70 @@
         home_copy.start()
         gs[...] += last
 
+    arrived(ga_recv, g_recv.at[1])
+    gh_send[...] = (gw[1 + core] + ga_recv[...].astype(F32)).astype(BF16)
+    homeward = remote(gh_send, gh_recv, g_send.at[3], g_recv.at[3], (grp, prv))
+    homeward.start()
+    sent += [pair_copy, homeward]
+
     for p in range(pieces):
         total = xs[p, rows_at(x, xrows), :].astype(F32)
-        for i in x_others:
-            arrived(x_recv.at[p, i], xs_recv.at[p, i])
-            total = total + x_recv[p, i].astype(F32)
+        arrived(x_recv.at[p], xs_recv.at[p])
+        for k in range(NX - 1):
+            total = total + x_recv[p, k].astype(F32)
         ys[p] = total.astype(BF16)
         for k, i in enumerate(y_others):
-            copy = remote(
-                ys.at[p, rows_at(i, yrows)], y_recv.at[p, y],
-                ys_send.at[p, k], ys_recv.at[p, y], at_y(i),
-            )
-            copy.start()
-            sent.append(copy)
-
-    arrived(ga_recv, g_recv.at[1])
-    gh_send[...] = (gw[1 + core] + ga_recv[...].astype(F32)).astype(BF16)
-    homeward = remote(gh_send, gh_recv, h_send.at[0], h_recv.at[0], (grp, prv))
-    homeward.start()
-    sent.append(homeward)
+            remote(
+                ys.at[p, rows_at(i, yrows)], y_recv.at[p, k], ys_send.at[p], ys_recv.at[p], at_y(i)
+            ).start()
+
+    @pl.when(even)
+    def _():
+        arrived(gb_recv, g_recv.at[0])
+        gw[0] = gw[0] + gb_recv[...].astype(F32)
 
     for p in range(pieces):
         total = ys[p, rows_at(y, yrows), :].astype(F32)
-        for i in y_others:
-            arrived(y_recv.at[p, i], ys_recv.at[p, i])
-            total = total + y_recv[p, i].astype(F32)
-        z_all[p, z] = total
+        arrived(y_recv.at[p], ys_recv.at[p])
+        for k in range(NY - 1):
+            total = total + y_recv[p, k].astype(F32)
+        z_all[p, 0] = total
         for k, i in enumerate(z_others):
-            copy = remote(
-                z_all.at[p, z], z_all.at[p, z], zs_send.at[p, k], zs_recv.at[p, z], at_z(i)
-            )
-            copy.start()
-            sent.append(copy)
+            remote(
+                z_all.at[p, 0], z_all.at[p, k + 1], zs_send.at[p], zs_recv.at[p], at_z(i)
+            ).start()
 
     @pl.when(even)
     def _():
         arrived(gs_recv, g_recv.at[2])
         gs[...] += gs_recv[...].astype(F32)
-        arrived(gb_recv, g_recv.at[0])
-        gw[0] = gw[0] + gb_recv[...].astype(F32)
 
     gs_copy = pltpu.make_async_copy(gs, gs_out, out_sem.at[0])
     gs_copy.start()
-
-    for p in range(pieces):
-        for i in z_others:
-            arrived(z_all.at[p, i], zs_recv.at[p, i])
-        total = z_all[p, 0]
-        for i in range(1, nz):
-            total = total + z_all[p, i]
-        piece = rel_all.at[core, p, x, y]
-        piece[...] = total.astype(BF16)
-        for k, i in enumerate(y_others):
-            copy = remote(piece, piece, ya_send.at[p, k], ya_recv.at[p, y], at_y(i))
-            copy.start()
-            sent.append(copy)
-
-    arrived(gh_recv, h_recv.at[0])
+    arrived(gh_recv, g_recv.at[3])
     gw[0] = gw[0] + gh_recv[...].astype(F32)
     gd_copy = pltpu.make_async_copy(gw.at[0], gd_out, out_sem.at[1])
     gd_copy.start()
 
     for p in range(pieces):
+        arrived(z_all.at[p, pl.ds(1, nz - 1)], zs_recv.at[p])
+        total = z_all[p, z]
+        for i in range(1, nz):
+            total = total + z_all[p, lax.rem(z + nz - i, nz)]
+        piece = rel_own.at[p, x, y]
+        piece[...] = total.astype(BF16)
         for i in y_others:
-            arrived(rel_all.at[core, p, x, i], ya_recv.at[p, i])
-        piece = rel_all.at[core, p, x]
-        for k, i in enumerate(x_others):
-            copy = remote(piece, piece, xa_send.at[p, k], xa_recv.at[p, x], at_x(i))
-            copy.start()
-            sent.append(copy)
-    for p in range(pieces):
+            remote(piece, piece, ya_send.at[p], ya_recv.at[p], at_y(i)).start()
+
+    for p in range(pieces):
+        arrived(rel_own.at[p, x, pl.ds(0, NY - 1)], ya_recv.at[p])
+        piece = rel_own.at[p, x]
         for i in x_others:
-            arrived(rel_all.at[core, p, i], xa_recv.at[p, i])
-        piece = rel_all.at[core, p]
-        copy = remote(piece, piece, ca_send.at[p], ca_recv.at[p], sib)
-        copy.start()
-        sent.append(copy)
-    rel_copies = []
-    for p in range(pieces):
-        arrived(rel_all.at[1 - core, p], ca_recv.at[p])
-        for h in range(2):
-            copy = pltpu.make_async_copy(
-                rel_all.at[h, p], rel_out.at[h, p], out_sem.at[2 + 2 * p + h]
-            )
-            copy.start()
-            rel_copies.append(copy)
+            remote(piece, piece, xa_send.at[p], xa_recv.at[p], at_x(i)).start()
+    for p in range(pieces):
+        arrived(rel_own.at[p, pl.ds(0, NX - 1)], xa_recv.at[p])
+        remote(rel_own.at[p], rel_out.at[core, p], ca_send.at[p], ca_recv.at[p], sib).start()
+        pltpu.make_async_copy(rel_own.at[p], rel_out.at[core, p], out_sem.at[2]).start()
 
     for copy in sent:
         copy.wait_send()
@@ -351,18 +331,27 @@
     @pl.when(even)
     def _():
         send_sib.wait_send()
-        for copy in far:
+        for copy in far[:2]:
             copy.wait_send()
+        arrived(idx, far_send.at[2])
         src_copy.wait_send()
 
     @pl.when(core == 1)
     def _():
         home_copy.wait_send()
 
+    for p in range(pieces):
+        arrived(x_recv.at[p], xs_send.at[p])
+        arrived(y_recv.at[p], ys_send.at[p])
+        arrived(z_all.at[p, pl.ds(1, nz - 1)], zs_send.at[p])
+        arrived(rel_own.at[p, x, pl.ds(0, NY - 1)], ya_send.at[p])
+        arrived(rel_own.at[p, pl.ds(0, NX - 1)], xa_send.at[p])
+        arrived(rel_own.at[p], ca_send.at[p])
     gs_copy.wait()
     gd_copy.wait()
-    for copy in rel_copies:
-        copy.wait()
+    arrived(rel_own, out_sem.at[2])
+    for p in range(pieces):
+        arrived(rel_out.at[1 - core, p], ca_recv.at[p])
 
 
 def store_kernel(
@@ -412,7 +401,7 @@
         block,
         vmem((rels, width), F32),
         vmem((rows_mm, width), F32),
-        vmem((width, rows_mm), BF16),
+        vmem((2 * width, rows_mm), BF16),
         vmem((width, ent), BF16),
         vmem((4, steps, ent), jnp.int32),
         vmem((4, steps, ent), jnp.int32),
@@ -421,7 +410,7 @@
         vmem((4, ent, ent), BF16),
         vmem((4, rows_mm, ent), BF16),
         vmem((4, width, ent), BF16),
-        vmem((4, width, ent), BF16),
+        vmem((4, width, ent), F32),
         vmem((4, width, ent), BF16),
         vmem((4, ent, 1), F32),
         vmem((4, ent, ent), BF16),
@@ -432,30 +421,18 @@
         block, block, block, block, block, block, block, block,
         vmem((pieces, prows, half), F32),
         vmem((pieces, prows, half), BF16),
-        vmem((pieces, NX, xrows, half), BF16),
+        vmem((pieces, NX - 1, xrows, half), BF16),
         vmem((pieces, xrows, half), BF16),
-        vmem((pieces, NY, CHUNK, half), BF16),
+        vmem((pieces, NY - 1, CHUNK, half), BF16),
         vmem((pieces, nz, CHUNK, half), F32),
-        vmem((2, pieces, NX, NY, CHUNK, half), BF16),
-        dma((8,)),
-        dma((2 + 2 * pieces,)),
-        dma((2,)),
-        dma((4,)),
-        dma((1,)),
-        dma((6,)),
-        dma((6,)),
+        vmem((pieces, NX, NY, CHUNK, half), BF16),
+        dma((5,)),
         dma((3,)),
         dma((3,)),
-        dma((1,)),
-        dma((1,)),
-        dma((pieces,)), dma((pieces,)),
-        dma((pieces, NX)), dma((pieces, NX)),
-        dma((pieces, NY)), dma((pieces, NY)),
-        dma((pieces, nz)), dma((pieces, nz)),
-        dma((pieces, NY)), dma((pieces, NY)),
-        dma((pieces, NX)), dma((pieces, NX)),
-        dma((pieces,)), dma((pieces,)),
-    ]
+        dma((4,)),
+        dma((3,)), dma((3,)),
+        dma((4,)), dma((4,)),
+    ] + [dma((pieces,))] * 14
     anywhere = pl.BlockSpec(memory_space=pl.ANY)
     grad = jax.ShapeDtypeStruct((ent, width), F32)
     grad_src, grad_dst, rel_parts = pl.pallas_call(
@@ -480,7 +457,7 @@
             vmem(rel_parts.shape, BF16), vmem((rels, width), F32),
             vmem((ent, width), F32), vmem((ent, width), F32), dma((3,)), dma((3,)),
         ],
-        compiler_params=pltpu.CompilerParams(vmem_limit_bytes=16 * 1024 * 1024),
+        compiler_params=pltpu.CompilerParams(vmem_limit_bytes=56 * 1024 * 1024),
     )(grad_src, grad_dst, rel_parts)
 
 

time: 67.1 us -> 62.4 us (0.930)
  local copies, waits for them, and re-layouts: 3.21 us -> 0 us
  Pallas kernels: 62.9 us -> 61.6 us
    unnamed x6 -> x0, local copies, waits for them, and re-layouts: 3.21 us -> none
    pallas_call x1, Pallas kernels: 61.2 us -> 58.9 us  [body(): pl.pallas_call(functools.partial(kernel, nz, rels, rows_mm, pieces), out_...]
    pallas_call x1, Pallas kernels: 1.69 us -> 2.7 us  [body(): pl.pallas_call(functools.partial(store_kernel, rels), out_shape=(grad, gr...]
where the time goes in v3:
time: 62.4 us; the launch traced here: 62.2 us
  Pallas kernels  61.6 us (99%)
  between operations  0.64 us (1%)
    pallas_call x1, Pallas kernels, body(): pl.pallas_call(functools.partial(kernel, nz, rels, rows_mm, pieces), out_...  58.9 us
    pallas_call x1, Pallas kernels, body(): pl.pallas_call(functools.partial(store_kernel, rels), out_shape=(grad, gr...  2.7 us

profile of v3, /device:TPU:1, one launch (start us, length us, event | category | flops | bytes accessed | tf_op | source)
XLA Modules:
  0.0 62.2 jit_solution(11250499486869306756)
XLA Ops:
  0.6 58.9 %shard_map.103 = (f32[512,256]{1,0:T(8,128)}, f32[512,256]{1,0:T(8,128)}, bf16[2,3,4,8,16,128]{5,4,3,2,1,0:T(8,128)(2,1)}) custom-call(bf16[512,256]{1,0:T(8,128)(2,1)} %src_hbm.1, bf16[512,256]{1,0:T(8,128)(2,1)} %dst_hbm.1, f32[1345,256]{1,0:T(8,128)} %rel_hbm.1, s32[4,512]{1,0:T(4,128)} %bitcast.7, s32[4,512]{1,0:T(4,128)} %bitcast.8, s32[4,512]{1,0:T(4,128)} %bitcast.9, ...), custom_call_target="tpu_custom_call" | custom-call | tf_op jit(solution)/shard_map/pallas_call | solution.py:438
  59.5 2.7 %shard_map.104 = (f32[512,256]{1,0:T(8,128)}, f32[512,256]{1,0:T(8,128)}, f32[1345,256]{1,0:T(8,128)}) custom-call(f32[512,256]{1,0:T(8,128)} %get-tuple-element.6.gs_in, f32[512,256]{1,0:T(8,128)} %get-tuple-element.7.gd_in, bf16[2,1536,128]{2,1,0:T(8,128)(2,1)} %bitcast.6), custom_call_target="tpu_custom_call" | custom-call | tf_op jit(solution)/shard_map/pallas_call | solution.py:451

commit v4 on v3

--- a/solution.py
+++ b/solution.py
@@ -30,7 +30,7 @@
     src_hbm, dst_hbm, rel_hbm, si_hbm, di_hbm, ri_hbm, ni_hbm, ec_hbm,
     gs_out, gd_out, rel_out,
     part, src_v, src_far, rel_v, rel_pad, rel_t, src_t, idx, idx_far, ec, ec_far,
-    ohs, ohr, sr, rr, qt, weight, pulls, back_v, gw, gs, gr,
+    ohs, ohr, sr, rr, qt, weight, pulls, back_v, value, gw, gs, gr,
     gs_send, gs_recv, ga_send, ga_recv, gb_send, gb_recv, gh_send, gh_recv,
     half_recv, xs, x_recv, ys, y_recv, z_all, rel_own,
     in_sem, out_sem, part_send, part_recv, far_send, far_recv,
@@ -77,34 +77,101 @@
     def arrived(buffer, recv):
         pltpu.make_async_copy(buffer, buffer, recv).wait()
 
+    own = [(si_hbm, 0), (di_hbm, 1), (ri_hbm, 2), (ni_hbm, 3)]
+    loads = [
+        pltpu.make_async_copy(ec_hbm, ec, in_sem.at[3]),
+        pltpu.make_async_copy(rel_hbm, rel_v, in_sem.at[0]),
+        pltpu.make_async_copy(src_hbm, src_v, in_sem.at[1]),
+        pltpu.make_async_copy(dst_hbm, part.at[0], in_sem.at[2]),
+    ]
+    for load in [pltpu.make_async_copy(ref, idx.at[k], in_sem.at[4]) for ref, k in own] + loads:
+        load.start()
     barrier = pltpu.get_barrier_semaphore()
     greet = [sib, (grp, nxt), (grp, prv)]
     greet += [at_x(i) for i in x_others] + [at_y(i) for i in y_others] + [at_z(i) for i in z_others]
     for device in greet:
         pl.semaphore_signal(barrier, inc=1, device_id=device, device_id_type=MESH)
-
-    own = [(si_hbm, 0), (di_hbm, 1), (ri_hbm, 2), (ni_hbm, 3)]
-    loads = [
-        pltpu.make_async_copy(rel_hbm, rel_v, in_sem.at[0]),
-        pltpu.make_async_copy(src_hbm, src_v, in_sem.at[1]),
-        pltpu.make_async_copy(dst_hbm, part.at[0], in_sem.at[2]),
-        pltpu.make_async_copy(ec_hbm, ec, in_sem.at[3]),
-    ]
-    for load in loads + [pltpu.make_async_copy(ref, idx.at[k], in_sem.at[4]) for ref, k in own]:
-        load.start()
     if rows_mm < pieces * prows:
         gr[:, rows_mm:, :] = jnp.zeros((2, pieces * prows - rows_mm, half), F32)
     tail = rels // 8 * 8
     rel_pad[tail:, :] = jnp.zeros((rows_mm - tail, width), F32)
-    for load in loads:
-        load.wait()
+
+    def tile_of(w):
+        if w in (0, 3):
+            return w
+        return jnp.where(even, 3 - w, w)
+
+    def row_of(k, w):
+        row = idx[k, pl.ds(tile_of(w), 1), :]
+        if w == 3:
+            row = jnp.where(even, idx_far[k, 3:4, :], row)
+        return row
+
+    def live_of(w):
+        counts = ec[...].astype(F32)
+        if w == 3:
+            counts = jnp.where(even, ec_far[...].astype(F32), counts)
+        place = lax.broadcasted_iota(jnp.int32, counts.shape, 1)
+        count = jnp.sum(jnp.where(place == tile_of(w), counts, 0.0), axis=1, keepdims=True)
+        slot = lax.broadcasted_iota(jnp.int32, (1, ent), 1).astype(F32)
+        return slot < count
+
+    def lanes(w):
+        return pl.ds(w * ent, ent)
+
+    def tables(w):
+        rows = lax.broadcasted_iota(jnp.int32, (ent, ent), 0)
+        ohs[:, lanes(w)] = (rows == jnp.where(live_of(w), row_of(0, w), -1)).astype(BF16)
+        chosen = (rows == row_of(3, w)).astype(F32)
+        weight[w] = jnp.sum(chosen, axis=1, keepdims=True) * (1.0 / ent)
+        rows = lax.broadcasted_iota(jnp.int32, (rows_mm, ent), 0)
+        ohr[:, lanes(w)] = (rows == row_of(2, w)).astype(BF16)
+
+    def gather(w):
+        picked = nn(src_t[...], ohs[:, lanes(w)])
+        both = nn(rel_t[...], ohr[:, lanes(w)])
+        scale = both[0:width] + both[width:]
+        sr[w] = picked.astype(BF16)
+        rr[w] = scale
+        qt[w] = (picked * scale).astype(BF16)
+
+    def finish(w, slot):
+        block = part[slot]
+        for low in range(0, ent, STEP):
+            scores = nn(block[low:low + STEP], qt[w])
+            rows = low + lax.broadcasted_iota(jnp.int32, (STEP, ent), 0)
+            decay = jnp.exp(jnp.minimum(-scores, 87.0))
+            share = weight[w, low:low + STEP]
+            share = jnp.where(rows == row_of(1, w), share - decay, share)
+            pulls[w, low:low + STEP] = (pl.reciprocal(1.0 + decay, approx=True) * share).astype(BF16)
+        pull = pulls[w]
+        dquery = nn(block.T, pull)
+        back_v[:, lanes(w)] = (dquery * rr[w]).astype(BF16)
+        value[:, lanes(w)] = (dquery * sr[w].astype(F32)).astype(BF16)
+
+    def grow(p, first, last):
+        low, high = p * prows, min((p + 1) * prows, rows_mm)
+        span = pl.ds(first * ent, (last - first) * ent)
+        grown = nt(ohr[low:high, span], value[:, span])
+        for h in range(2):
+            grown_half = grown[:, h * half:(h + 1) * half]
+            if first == 0:
+                gr[h, low:high, :] = grown_half
+            else:
+                gr[h, low:high, :] += grown_half
+
+    swaps = [
+        remote(
+            gr.at[1 - core, pl.ds(p * prows, prows)], half_recv.at[p],
+            s_send.at[p], s_recv.at[p], sib,
+        )
+        for p in range(pieces)
+    ]
+
     arrived(idx, in_sem.at[4])
-    rel_pad[0:rels, :] = rel_v[...]
-    turned = rel_pad[...].T
-    high = turned.astype(BF16)
-    rel_t[0:width, :] = high
-    rel_t[width:, :] = (turned - high.astype(F32)).astype(BF16)
-    src_t[...] = src_v[...].T
+    loads[0].wait()
+    for w in range(3):
+        tables(w)
 
     pl.semaphore_wait(barrier, len(greet))
 
@@ -127,81 +194,31 @@
         for copy in far:
             copy.start()
 
-    def tile_of(w):
-        if w in (0, 3):
-            return w
-        return jnp.where(even, 3 - w, w)
-
-    def row_of(k, w):
-        row = idx[k, pl.ds(tile_of(w), 1), :]
-        if w == 3:
-            row = jnp.where(even, idx_far[k, 3:4, :], row)
-        return row
-
-    def live_of(w):
-        counts = ec[...].astype(F32)
-        if w == 3:
-            counts = jnp.where(even, ec_far[...].astype(F32), counts)
-        place = lax.broadcasted_iota(jnp.int32, counts.shape, 1)
-        count = jnp.sum(jnp.where(place == tile_of(w), counts, 0.0), axis=1, keepdims=True)
-        slot = lax.broadcasted_iota(jnp.int32, (1, ent), 1).astype(F32)
-        return slot < count
-
-    def prepare(w):
-        rows = lax.broadcasted_iota(jnp.int32, (ent, ent), 0)
-        ohs[w] = (rows == jnp.where(live_of(w), row_of(0, w), -1)).astype(BF16)
-        chosen = (rows == row_of(3, w)).astype(F32)
-        weight[w] = jnp.sum(chosen, axis=1, keepdims=True) * (1.0 / ent)
-        rows = lax.broadcasted_iota(jnp.int32, (rows_mm, ent), 0)
-        ohr[w] = (rows == row_of(2, w)).astype(BF16)
-        picked = nn(src_t[...], ohs[w])
-        both = nn(rel_t[...], ohr[w])
-        scale = both[0:width] + both[width:]
-        sr[w] = picked.astype(BF16)
-        rr[w] = scale
-        qt[w] = (picked * scale).astype(BF16)
-
-    def finish(w, slot):
-        block = part[slot]
-        for low in range(0, ent, STEP):
-            scores = nn(block[low:low + STEP], qt[w])
-            rows = low + lax.broadcasted_iota(jnp.int32, (STEP, ent), 0)
-            decay = jnp.exp(jnp.minimum(-scores, 87.0))
-            share = weight[w, low:low + STEP]
-            share = jnp.where(rows == row_of(1, w), share - decay, share)
-            pulls[w, low:low + STEP] = (pl.reciprocal(1.0 + decay, approx=True) * share).astype(BF16)
-        pull = pulls[w]
-        dquery = nn(block.T, pull)
-        back_v[w] = (dquery * rr[w]).astype(BF16)
-        value = (dquery * sr[w].astype(F32)).astype(BF16)
-        for p in range(pieces):
-            low, high = p * prows, min((p + 1) * prows, rows_mm)
-            grown = nt(ohr[w, low:high, :], value)
-            for h in range(2):
-                grown_half = grown[:, h * half:(h + 1) * half]
-                if w == 0:
-                    gr[h, low:high, :] = grown_half
-                else:
-                    gr[h, low:high, :] += grown_half
-            if w == 3:
-                swaps[p].start()
-
-    def spread(w):
-        gw[w] = nt(pulls[w], qt[w])
-        return nt(ohs[w], back_v[w])
-
-    swaps = [
-        remote(
-            gr.at[1 - core, pl.ds(p * prows, prows)], half_recv.at[p],
-            s_send.at[p], s_recv.at[p], sib,
-        )
-        for p in range(pieces)
-    ]
-
-    prepare(0)
+    for load in loads[1:]:
+        load.wait()
+    rel_pad[0:rels, :] = rel_v[...]
+    turned = rel_pad[...].T
+    high = turned.astype(BF16)
+    rel_t[0:width, :] = high
+    rel_t[width:, :] = (turned - high.astype(F32)).astype(BF16)
+    src_t[...] = src_v[...].T
+
+    gather(0)
     finish(0, 0)
-    prepare(1)
-    prepare(2)
+    for p in range(pieces):
+        grow(p, 0, 1)
+    gather(1)
+    gather(2)
+
+    @pl.when(even)
+    def _():
+        arrived(idx_far, far_recv.at[2])
+        arrived(ec_far, far_recv.at[1])
+        arrived(src_far, far_recv.at[0])
+        src_t[...] = src_far[...].T
+
+    tables(3)
+    gather(3)
 
     arrived(part.at[direct], part_recv.at[direct])
     forward = remote(
@@ -209,30 +226,26 @@
     )
     forward.start()
 
-    @pl.when(even)
-    def _():
-        arrived(idx_far, far_recv.at[2])
-        arrived(ec_far, far_recv.at[1])
-        arrived(src_far, far_recv.at[0])
-        src_t[...] = src_far[...].T
-
     @pl.when(core == 1)
     def _():
         arrived(part.at[3], part_recv.at[3])
 
-    prepare(3)
     finish(1, 2 + core)
     other = 1 + core
     arrived(part.at[other], part_recv.at[other])
     finish(2, 1)
     finish(3, 1 + core)
+    for p in range(pieces):
+        grow(p, 1, 4)
+        swaps[p].start()
 
     sent = [send_next, forward] + swaps
 
     def rows_at(i, size):
         return pl.ds(pl.multiple_of(i * size, size), size)
 
-    gs[...] = spread(0) + spread(1)
+    for w in range(3):
+        gw[w] = nt(pulls[w], qt[w])
     for p in range(pieces):
         arrived(half_recv.at[p], s_recv.at[p])
         xs[p] = (gr[core, p * prows:(p + 1) * prows, :] + half_recv[p]).astype(BF16)
@@ -241,8 +254,10 @@
                 xs.at[p, rows_at(i, xrows)], x_recv.at[p, k], xs_send.at[p], xs_recv.at[p], at_x(i)
             ).start()
 
-    gs[...] += spread(2)
-    last = spread(3)
+    own_slots = pl.ds(0, 3 * ent)
+    gs[...] = nt(ohs[:, own_slots], back_v[:, own_slots])
+    last = nt(ohs[:, lanes(3)], back_v[:, lanes(3)])
+    gw[3] = nt(pulls[3], qt[3])
     ga_send[...] = (gw[3] + jnp.where(even, gw[2], 0.0)).astype(BF16)
     pair_copy = remote(ga_send, ga_recv, g_send.at[1], g_recv.at[1], sib)
     pair_copy.start()
@@ -357,28 +372,28 @@
 def store_kernel(
     rels, gs_in, gd_in, rel_in, gs_out, gd_out, rel_out, rel_b, rel_f, gs_v, gd_v, in_sem, out_sem
 ):
-    ins = [
+    loads = [
         pltpu.make_async_copy(rel_in, rel_b, in_sem.at[0]),
         pltpu.make_async_copy(gs_in, gs_v, in_sem.at[1]),
         pltpu.make_async_copy(gd_in, gd_v, in_sem.at[2]),
     ]
-    outs = [
+    stores = [
         pltpu.make_async_copy(rel_f, rel_out, out_sem.at[0]),
         pltpu.make_async_copy(gs_v, gs_out, out_sem.at[1]),
         pltpu.make_async_copy(gd_v, gd_out, out_sem.at[2]),
     ]
-    for copy in ins:
-        copy.start()
+    for load in loads:
+        load.start()
     half = rel_b.shape[2]
-    ins[0].wait()
+    loads[0].wait()
     for h in range(2):
         rel_f[:, h * half:(h + 1) * half] = rel_b[h, 0:rels, :].astype(F32)
-    outs[0].start()
+    stores[0].start()
     for k in (1, 2):
-        ins[k].wait()
-        outs[k].start()
-    for copy in outs:
-        copy.wait()
+        loads[k].wait()
+        stores[k].start()
+    for store in stores:
+        store.wait()
 
 
 def body(src_embed, dst_embed, relation, src_index, dst_index, rel_index, neg_index, edge_count):
@@ -407,14 +422,15 @@
         vmem((4, steps, ent), jnp.int32),
         vmem((1, steps), jnp.int32),
         vmem((1, steps), jnp.int32),
-        vmem((4, ent, ent), BF16),
-        vmem((4, rows_mm, ent), BF16),
+        vmem((ent, 4 * ent), BF16),
+        vmem((rows_mm, 4 * ent), BF16),
         vmem((4, width, ent), BF16),
         vmem((4, width, ent), F32),
         vmem((4, width, ent), BF16),
         vmem((4, ent, 1), F32),
         vmem((4, ent, ent), BF16),
-        vmem((4, width, ent), BF16),
+        vmem((width, 4 * ent), BF16),
+        vmem((width, 4 * ent), BF16),
         vmem((4, ent, width), F32),
         vmem((ent, width), F32),
         vmem((2, pieces * prows, half), F32),

time: 62.4 us -> 64.2 us (1.029)
  Pallas kernels: 61.6 us -> 63.3 us
    pallas_call x1, Pallas kernels: 58.9 us -> 60.6 us  [body(): pl.pallas_call(functools.partial(kernel, nz, rels, rows_mm, pieces), out_...]
where the time goes in v4:
time: 64.2 us; the launch traced here: 64.1 us
  Pallas kernels  63.3 us (99%)
  between operations  0.8 us (1%)
    pallas_call x1, Pallas kernels, body(): pl.pallas_call(functools.partial(kernel, nz, rels, rows_mm, pieces), out_...  60.6 us
    pallas_call x1, Pallas kernels, body(): pl.pallas_call(functools.partial(store_kernel, rels), out_shape=(grad, gr...  2.7 us

profile of v4, /device:TPU:1, one launch (start us, length us, event | category | flops | bytes accessed | tf_op | source)
XLA Modules:
  0.0 64.1 jit_solution(5922004339241165019)
XLA Ops:
  0.6 60.6 %shard_map.103 = (f32[512,256]{1,0:T(8,128)}, f32[512,256]{1,0:T(8,128)}, bf16[2,3,4,8,16,128]{5,4,3,2,1,0:T(8,128)(2,1)}) custom-call(bf16[512,256]{1,0:T(8,128)(2,1)} %src_hbm.1, bf16[512,256]{1,0:T(8,128)(2,1)} %dst_hbm.1, f32[1345,256]{1,0:T(8,128)} %rel_hbm.1, s32[4,512]{1,0:T(4,128)} %bitcast.7, s32[4,512]{1,0:T(4,128)} %bitcast.8, s32[4,512]{1,0:T(4,128)} %bitcast.9, ...), custom_call_target="tpu_custom_call" | custom-call | tf_op jit(solution)/shard_map/pallas_call | solution.py:454
  61.2 2.7 %shard_map.104 = (f32[512,256]{1,0:T(8,128)}, f32[512,256]{1,0:T(8,128)}, f32[1345,256]{1,0:T(8,128)}) custom-call(f32[512,256]{1,0:T(8,128)} %get-tuple-element.6.gs_in, f32[512,256]{1,0:T(8,128)} %get-tuple-element.7.gd_in, bf16[2,1536,128]{2,1,0:T(8,128)(2,1)} %bitcast.6), custom_call_target="tpu_custom_call" | custom-call | tf_op jit(solution)/shard_map/pallas_call | solution.py:467

commit v5 on v4

--- a/solution.py
+++ b/solution.py
@@ -64,9 +64,11 @@
     def at_z(i):
         return ((i // ZLO) * NX + x, lax.rem(i, ZLO) * NY * 2 + y * 2 + core)
 
-    x_others = [lax.rem(x + k, NX) for k in range(1, NX)]
-    y_others = [lax.rem(y + k, NY) for k in range(1, NY)]
-    z_others = [lax.rem(z + k, nz) for k in range(1, nz)]
+    def ring(place, size):
+        steps = sorted(range(1, size), key=lambda k: -min(k, size - k))
+        return [(k, lax.rem(place + k, size)) for k in steps]
+
+    x_others, y_others, z_others = ring(x, NX), ring(y, NY), ring(z, nz)
 
     def remote(source, target, send, recv, device):
         return pltpu.make_async_remote_copy(
@@ -80,15 +82,17 @@
     own = [(si_hbm, 0), (di_hbm, 1), (ri_hbm, 2), (ni_hbm, 3)]
     loads = [
         pltpu.make_async_copy(ec_hbm, ec, in_sem.at[3]),
+        pltpu.make_async_copy(dst_hbm, part.at[0], in_sem.at[2]),
+        pltpu.make_async_copy(src_hbm, src_v, in_sem.at[1]),
         pltpu.make_async_copy(rel_hbm, rel_v, in_sem.at[0]),
-        pltpu.make_async_copy(src_hbm, src_v, in_sem.at[1]),
-        pltpu.make_async_copy(dst_hbm, part.at[0], in_sem.at[2]),
     ]
-    for load in [pltpu.make_async_copy(ref, idx.at[k], in_sem.at[4]) for ref, k in own] + loads:
+    tables_in = [pltpu.make_async_copy(ref, idx.at[k], in_sem.at[4]) for ref, k in own]
+    for load in loads[:2] + tables_in + loads[2:]:
         load.start()
     barrier = pltpu.get_barrier_semaphore()
     greet = [sib, (grp, nxt), (grp, prv)]
-    greet += [at_x(i) for i in x_others] + [at_y(i) for i in y_others] + [at_z(i) for i in z_others]
+    greet += [at_x(i) for _, i in x_others] + [at_y(i) for _, i in y_others]
+    greet += [at_z(i) for _, i in z_others]
     for device in greet:
         pl.semaphore_signal(barrier, inc=1, device_id=device, device_id_type=MESH)
     if rows_mm < pieces * prows:
@@ -135,19 +139,29 @@
         rr[w] = scale
         qt[w] = (picked * scale).astype(BF16)
 
-    def finish(w, slot):
-        block = part[slot]
-        for low in range(0, ent, STEP):
-            scores = nn(block[low:low + STEP], qt[w])
-            rows = low + lax.broadcasted_iota(jnp.int32, (STEP, ent), 0)
+    def score(w, slot, h):
+        mid = ent // 2
+        for low in range(h * mid, (h + 1) * mid, min(STEP, mid)):
+            size = min(STEP, mid)
+            scores = nn(part[slot, low:low + size, :], qt[w])
+            rows = low + lax.broadcasted_iota(jnp.int32, (size, ent), 0)
             decay = jnp.exp(jnp.minimum(-scores, 87.0))
-            share = weight[w, low:low + STEP]
+            share = weight[w, low:low + size]
             share = jnp.where(rows == row_of(1, w), share - decay, share)
-            pulls[w, low:low + STEP] = (pl.reciprocal(1.0 + decay, approx=True) * share).astype(BF16)
-        pull = pulls[w]
-        dquery = nn(block.T, pull)
+            inverse = pl.reciprocal(1.0 + decay, approx=True)
+            pulls[w, low:low + size] = (inverse * share).astype(BF16)
+
+    def pull_half(w, slot, h):
+        return nn(part[slot, halves[h], :].T, pulls[w, halves[h], :])
+
+    def give(w, dquery):
         back_v[:, lanes(w)] = (dquery * rr[w]).astype(BF16)
         value[:, lanes(w)] = (dquery * sr[w].astype(F32)).astype(BF16)
+
+    def finish(w, slot):
+        score(w, slot, 0)
+        score(w, slot, 1)
+        give(w, nn(part[slot].T, pulls[w]))
 
     def grow(p, first, last):
         low, high = p * prows, min((p + 1) * prows, rows_mm)
@@ -176,11 +190,24 @@
     pl.semaphore_wait(barrier, len(greet))
 
     direct = 2 - core
-    send_next = remote(
-        dst_hbm, part.at[direct], part_send.at[0], part_recv.at[direct], (grp, nxt)
-    )
-    send_next.start()
-    send_sib = remote(dst_hbm, part.at[3], part_send.at[1], part_recv.at[3], sib)
+    other = 1 + core
+    halves = [pl.ds(0, ent // 2), pl.ds(ent // 2, ent // 2)]
+
+    def send_part(source, slot, h, send, device):
+        return remote(
+            source.at[halves[h]], part.at[slot, halves[h]], part_send.at[send, h],
+            part_recv.at[slot, h], device,
+        )
+
+    def arrived_part(slot, h):
+        arrived(part.at[slot, halves[h]], part_recv.at[slot, h])
+
+    send_next = [send_part(part.at[0], direct, h, 0, (grp, nxt)) for h in range(2)]
+    send_sib = [send_part(part.at[0], 3, h, 1, sib) for h in range(2)]
+    forward = [send_part(part.at[direct], direct, h, 2, sib) for h in range(2)]
+    loads[1].wait()
+    for copy in send_next:
+        copy.start()
     far = [remote(src_hbm, src_far, far_send.at[0], far_recv.at[0], (grp, prv))]
     far += [remote(ec_hbm, ec_far, far_send.at[1], far_recv.at[1], (grp, prv))]
     far += [
@@ -190,11 +217,10 @@
 
     @pl.when(even)
     def _():
-        send_sib.start()
-        for copy in far:
+        for copy in send_sib + far:
             copy.start()
 
-    for load in loads[1:]:
+    for load in loads[2:]:
         load.wait()
     rel_pad[0:rels, :] = rel_v[...]
     turned = rel_pad[...].T
@@ -205,8 +231,6 @@
 
     gather(0)
     finish(0, 0)
-    for p in range(pieces):
-        grow(p, 0, 1)
     gather(1)
     gather(2)
 
@@ -220,66 +244,77 @@
     tables(3)
     gather(3)
 
-    arrived(part.at[direct], part_recv.at[direct])
-    forward = remote(
-        part.at[direct], part.at[direct], part_send.at[2], part_recv.at[direct], sib
-    )
-    forward.start()
+    for h in range(2):
+        arrived_part(direct, h)
+        forward[h].start()
 
     @pl.when(core == 1)
     def _():
-        arrived(part.at[3], part_recv.at[3])
+        arrived_part(3, 0)
+        arrived_part(3, 1)
 
     finish(1, 2 + core)
-    other = 1 + core
-    arrived(part.at[other], part_recv.at[other])
-    finish(2, 1)
-    finish(3, 1 + core)
-    for p in range(pieces):
-        grow(p, 1, 4)
+    for p in range(pieces):
+        grow(p, 0, 2)
+    arrived_part(other, 0)
+    score(2, 1, 0)
+    score(3, other, 0)
+    first = [pull_half(2, 1, 0), pull_half(3, other, 0)]
+    arrived_part(other, 1)
+    score(2, 1, 1)
+    score(3, other, 1)
+    give(2, first[0] + pull_half(2, 1, 1))
+    give(3, first[1] + pull_half(3, other, 1))
+    for p in range(pieces):
+        grow(p, 2, 4)
         swaps[p].start()
 
-    sent = [send_next, forward] + swaps
+    sent = send_next + forward + swaps
 
     def rows_at(i, size):
         return pl.ds(pl.multiple_of(i * size, size), size)
 
-    for w in range(3):
+    for w in (2, 3):
         gw[w] = nt(pulls[w], qt[w])
-    for p in range(pieces):
-        arrived(half_recv.at[p], s_recv.at[p])
-        xs[p] = (gr[core, p * prows:(p + 1) * prows, :] + half_recv[p]).astype(BF16)
-        for k, i in enumerate(x_others):
-            remote(
-                xs.at[p, rows_at(i, xrows)], x_recv.at[p, k], xs_send.at[p], xs_recv.at[p], at_x(i)
-            ).start()
-
-    own_slots = pl.ds(0, 3 * ent)
-    gs[...] = nt(ohs[:, own_slots], back_v[:, own_slots])
-    last = nt(ohs[:, lanes(3)], back_v[:, lanes(3)])
-    gw[3] = nt(pulls[3], qt[3])
     ga_send[...] = (gw[3] + jnp.where(even, gw[2], 0.0)).astype(BF16)
     pair_copy = remote(ga_send, ga_recv, g_send.at[1], g_recv.at[1], sib)
     pair_copy.start()
+    last = nt(ohs[:, lanes(3)], back_v[:, lanes(3)])
     gs_send[...] = last.astype(BF16)
     src_copy = remote(gs_send, gs_recv, g_send.at[2], g_recv.at[2], (grp, nxt))
+
+    @pl.when(even)
+    def _():
+        src_copy.start()
+
+    gw[1] = nt(pulls[1], qt[1])
     gb_send[...] = gw[1].astype(BF16)
     home_copy = remote(gb_send, gb_recv, g_send.at[0], g_recv.at[0], sib)
 
-    @pl.when(even)
-    def _():
-        src_copy.start()
-
     @pl.when(core == 1)
     def _():
         home_copy.start()
-        gs[...] += last
+
+    for p in range(pieces):
+        arrived(half_recv.at[p], s_recv.at[p])
+        xs[p] = (gr[core, p * prows:(p + 1) * prows, :] + half_recv[p]).astype(BF16)
+        for k, i in x_others:
+            remote(
+                xs.at[p, rows_at(i, xrows)], x_recv.at[p, k - 1], xs_send.at[p], xs_recv.at[p], at_x(i)
+            ).start()
 
     arrived(ga_recv, g_recv.at[1])
     gh_send[...] = (gw[1 + core] + ga_recv[...].astype(F32)).astype(BF16)
     homeward = remote(gh_send, gh_recv, g_send.at[3], g_recv.at[3], (grp, prv))
     homeward.start()
     sent += [pair_copy, homeward]
+    gw[0] = nt(pulls[0], qt[0])
+    own_slots = pl.ds(0, 3 * ent)
+    gs[...] = nt(ohs[:, own_slots], back_v[:, own_slots])
+
+    @pl.when(core == 1)
+    def _():
+        gs[...] += last
 
     for p in range(pieces):
         total = xs[p, rows_at(x, xrows), :].astype(F32)
@@ -287,15 +322,10 @@
         for k in range(NX - 1):
             total = total + x_recv[p, k].astype(F32)
         ys[p] = total.astype(BF16)
-        for k, i in enumerate(y_others):
+        for k, i in y_others:
             remote(
-                ys.at[p, rows_at(i, yrows)], y_recv.at[p, k], ys_send.at[p], ys_recv.at[p], at_y(i)
+                ys.at[p, rows_at(i, yrows)], y_recv.at[p, k - 1], ys_send.at[p], ys_recv.at[p], at_y(i)
             ).start()
-
-    @pl.when(even)
-    def _():
-        arrived(gb_recv, g_recv.at[0])
-        gw[0] = gw[0] + gb_recv[...].astype(F32)
 
     for p in range(pieces):
         total = ys[p, rows_at(y, yrows), :].astype(F32)
@@ -303,15 +333,17 @@
         for k in range(NY - 1):
             total = total + y_recv[p, k].astype(F32)
         z_all[p, 0] = total
-        for k, i in enumerate(z_others):
+        for k, i in z_others:
             remote(
-                z_all.at[p, 0], z_all.at[p, k + 1], zs_send.at[p], zs_recv.at[p], at_z(i)
+                z_all.at[p, 0], z_all.at[p, k], zs_send.at[p], zs_recv.at[p], at_z(i)
             ).start()
 
     @pl.when(even)
     def _():
         arrived(gs_recv, g_recv.at[2])
         gs[...] += gs_recv[...].astype(F32)
+        arrived(gb_recv, g_recv.at[0])
+        gw[0] = gw[0] + gb_recv[...].astype(F32)
 
     gs_copy = pltpu.make_async_copy(gs, gs_out, out_sem.at[0])
     gs_copy.start()
@@ -327,13 +359,13 @@
             total = total + z_all[p, lax.rem(z + nz - i, nz)]
         piece = rel_own.at[p, x, y]
         piece[...] = total.astype(BF16)
-        for i in y_others:
+        for _, i in y_others:
             remote(piece, piece, ya_send.at[p], ya_recv.at[p], at_y(i)).start()
 
     for p in range(pieces):
         arrived(rel_own.at[p, x, pl.ds(0, NY - 1)], ya_recv.at[p])
         piece = rel_own.at[p, x]
-        for i in x_others:
+        for _, i in x_others:
             remote(piece, piece, xa_send.at[p], xa_recv.at[p], at_x(i)).start()
     for p in range(pieces):
         arrived(rel_own.at[p, pl.ds(0, NX - 1)], xa_recv.at[p])
@@ -345,8 +377,7 @@
 
     @pl.when(even)
     def _():
-        send_sib.wait_send()
-        for copy in far[:2]:
+        for copy in send_sib + far[:2]:
             copy.wait_send()
         arrived(idx, far_send.at[2])
         src_copy.wait_send()
@@ -444,8 +475,8 @@
         vmem((pieces, NX, NY, CHUNK, half), BF16),
         dma((5,)),
         dma((3,)),
-        dma((3,)),
-        dma((4,)),
+        dma((3, 2)),
+        dma((4, 2)),
         dma((3,)), dma((3,)),
         dma((4,)), dma((4,)),
     ] + [dma((pieces,))] * 14

time: 64.2 us -> 62.1 us (0.967)
  Pallas kernels: 63.3 us -> 61.1 us
    pallas_call x1, Pallas kernels: 60.6 us -> 58.4 us  [body(): pl.pallas_call(functools.partial(kernel, nz, rels, rows_mm, pieces), out_...]
where the time goes in v5:
time: 62.1 us; the launch traced here: 61.9 us
  Pallas kernels  61.1 us (98%)
  between operations  0.8 us (1%)
    pallas_call x1, Pallas kernels, body(): pl.pallas_call(functools.partial(kernel, nz, rels, rows_mm, pieces), out_...  58.4 us
    pallas_call x1, Pallas kernels, body(): pl.pallas_call(functools.partial(store_kernel, rels), out_shape=(grad, gr...  2.7 us

profile of v5, /device:TPU:1, one launch (start us, length us, event | category | flops | bytes accessed | tf_op | source)
XLA Modules:
  0.0 61.9 jit_solution(16265079316023174163)
XLA Ops:
  0.6 58.4 %shard_map.103 = (f32[512,256]{1,0:T(8,128)}, f32[512,256]{1,0:T(8,128)}, bf16[2,3,4,8,16,128]{5,4,3,2,1,0:T(8,128)(2,1)}) custom-call(bf16[512,256]{1,0:T(8,128)(2,1)} %src_hbm.1, bf16[512,256]{1,0:T(8,128)(2,1)} %dst_hbm.1, f32[1345,256]{1,0:T(8,128)} %rel_hbm.1, s32[4,512]{1,0:T(4,128)} %bitcast.7, s32[4,512]{1,0:T(4,128)} %bitcast.8, s32[4,512]{1,0:T(4,128)} %bitcast.9, ...), custom_call_target="tpu_custom_call" | custom-call | tf_op jit(solution)/shard_map/pallas_call | solution.py:485
  59.1 2.7 %shard_map.104 = (f32[512,256]{1,0:T(8,128)}, f32[512,256]{1,0:T(8,128)}, f32[1345,256]{1,0:T(8,128)}) custom-call(f32[512,256]{1,0:T(8,128)} %get-tuple-element.6.gs_in, f32[512,256]{1,0:T(8,128)} %get-tuple-element.7.gd_in, bf16[2,1536,128]{2,1,0:T(8,128)(2,1)} %bitcast.6), custom_call_target="tpu_custom_call" | custom-call | tf_op jit(solution)/shard_map/pallas_call | solution.py:498

commit v6 on v5

--- a/solution.py
+++ b/solution.py
@@ -34,7 +34,7 @@
     gs_send, gs_recv, ga_send, ga_recv, gb_send, gb_recv, gh_send, gh_recv,
     half_recv, xs, x_recv, ys, y_recv, z_all, rel_own,
     in_sem, out_sem, part_send, part_recv, far_send, far_recv,
-    g_send, g_recv, s_send, s_recv,
+    g_send, g_recv, h_send, h_recv, h_out, s_send, s_recv,
     xs_send, xs_recv, ys_send, ys_recv, zs_send, zs_recv,
     ya_send, ya_recv, xa_send, xa_recv, ca_send, ca_recv,
 ):
@@ -231,6 +231,8 @@
 
     gather(0)
     finish(0, 0)
+    for p in range(pieces):
+        grow(p, 0, 1)
     gather(1)
     gather(2)
 
@@ -255,7 +257,7 @@
 
     finish(1, 2 + core)
     for p in range(pieces):
-        grow(p, 0, 2)
+        grow(p, 1, 2)
     arrived_part(other, 0)
     score(2, 1, 0)
     score(3, other, 0)
@@ -305,9 +307,7 @@
 
     arrived(ga_recv, g_recv.at[1])
     gh_send[...] = (gw[1 + core] + ga_recv[...].astype(F32)).astype(BF16)
-    homeward = remote(gh_send, gh_recv, g_send.at[3], g_recv.at[3], (grp, prv))
-    homeward.start()
-    sent += [pair_copy, homeward]
+    sent.append(pair_copy)
     gw[0] = nt(pulls[0], qt[0])
     own_slots = pl.ds(0, 3 * ent)
     gs[...] = nt(ohs[:, own_slots], back_v[:, own_slots])
@@ -347,11 +347,6 @@
 
     gs_copy = pltpu.make_async_copy(gs, gs_out, out_sem.at[0])
     gs_copy.start()
-    arrived(gh_recv, g_recv.at[3])
-    gw[0] = gw[0] + gh_recv[...].astype(F32)
-    gd_copy = pltpu.make_async_copy(gw.at[0], gd_out, out_sem.at[1])
-    gd_copy.start()
-
     for p in range(pieces):
         arrived(z_all.at[p, pl.ds(1, nz - 1)], zs_recv.at[p])
         total = z_all[p, z]
@@ -367,10 +362,26 @@
         piece = rel_own.at[p, x]
         for _, i in x_others:
             remote(piece, piece, xa_send.at[p], xa_recv.at[p], at_x(i)).start()
+    homeward = [
+        remote(gh_send.at[part_rows], gh_recv.at[part_rows], h_send.at[h], h_recv.at[h], (grp, prv))
+        for h, part_rows in enumerate(halves)
+    ]
+    for copy in homeward:
+        copy.start()
+    sent += homeward
     for p in range(pieces):
         arrived(rel_own.at[p, pl.ds(0, NX - 1)], xa_recv.at[p])
         remote(rel_own.at[p], rel_out.at[core, p], ca_send.at[p], ca_recv.at[p], sib).start()
         pltpu.make_async_copy(rel_own.at[p], rel_out.at[core, p], out_sem.at[2]).start()
+
+    gd_copies = []
+    for h, part_rows in enumerate(halves):
+        arrived(gh_recv.at[part_rows], h_recv.at[h])
+        gw[0, part_rows, :] = gw[0, part_rows, :] + gh_recv[part_rows, :].astype(F32)
+        gd_copies.append(
+            pltpu.make_async_copy(gw.at[0, part_rows], gd_out.at[part_rows], h_out.at[h])
+        )
+        gd_copies[h].start()
 
     for copy in sent:
         copy.wait_send()
@@ -394,7 +405,8 @@
         arrived(rel_own.at[p, pl.ds(0, NX - 1)], xa_send.at[p])
         arrived(rel_own.at[p], ca_send.at[p])
     gs_copy.wait()
-    gd_copy.wait()
+    for copy in gd_copies:
+        copy.wait()
     arrived(rel_own, out_sem.at[2])
     for p in range(pieces):
         arrived(rel_out.at[1 - core, p], ca_recv.at[p])
@@ -403,28 +415,33 @@
 def store_kernel(
     rels, gs_in, gd_in, rel_in, gs_out, gd_out, rel_out, rel_b, rel_f, gs_v, gd_v, in_sem, out_sem
 ):
+    pieces, rows, half = rel_b.shape[1:]
+    spans = [(p * rows, min((p + 1) * rows, rels)) for p in range(pieces)]
     loads = [
-        pltpu.make_async_copy(rel_in, rel_b, in_sem.at[0]),
-        pltpu.make_async_copy(gs_in, gs_v, in_sem.at[1]),
-        pltpu.make_async_copy(gd_in, gd_v, in_sem.at[2]),
-    ]
-    stores = [
-        pltpu.make_async_copy(rel_f, rel_out, out_sem.at[0]),
-        pltpu.make_async_copy(gs_v, gs_out, out_sem.at[1]),
-        pltpu.make_async_copy(gd_v, gd_out, out_sem.at[2]),
+        pltpu.make_async_copy(rel_in.at[h, p], rel_b.at[h, p], in_sem.at[2 + 2 * p + h])
+        for p in range(pieces) for h in range(2)
+    ] + [
+        pltpu.make_async_copy(gs_in, gs_v, in_sem.at[0]),
+        pltpu.make_async_copy(gd_in, gd_v, in_sem.at[1]),
     ]
     for load in loads:
         load.start()
-    half = rel_b.shape[2]
-    loads[0].wait()
-    for h in range(2):
-        rel_f[:, h * half:(h + 1) * half] = rel_b[h, 0:rels, :].astype(F32)
-    stores[0].start()
-    for k in (1, 2):
-        loads[k].wait()
-        stores[k].start()
-    for store in stores:
-        store.wait()
+    stores = []
+
+    def store(source, target):
+        stores.append(pltpu.make_async_copy(source, target, out_sem.at[len(stores)]))
+        stores[-1].start()
+
+    for p, (low, high) in enumerate(spans):
+        for h in range(2):
+            loads[2 * p + h].wait()
+            rel_f[low:high, h * half:(h + 1) * half] = rel_b[h, p, 0:high - low, :].astype(F32)
+        store(rel_f.at[low:high], rel_out.at[low:high])
+    for load, source, target in ((loads[-2], gs_v, gs_out), (loads[-1], gd_v, gd_out)):
+        load.wait()
+        store(source, target)
+    for copy in stores:
+        copy.wait()
 
 
 def body(src_embed, dst_embed, relation, src_index, dst_index, rel_index, neg_index, edge_count):
@@ -478,7 +495,8 @@
         dma((3, 2)),
         dma((4, 2)),
         dma((3,)), dma((3,)),
-        dma((4,)), dma((4,)),
+        dma((3,)), dma((3,)),
+        dma((2,)), dma((2,)), dma((2,)),
     ] + [dma((pieces,))] * 14
     anywhere = pl.BlockSpec(memory_space=pl.ANY)
     grad = jax.ShapeDtypeStruct((ent, width), F32)
@@ -494,7 +512,7 @@
             collective_id=0, has_side_effects=True, vmem_limit_bytes=56 * 1024 * 1024
         ),
     )(src_embed, dst_embed, relation, *tables, edge_count.reshape(1, steps))
-    rel_parts = rel_parts.reshape(2, pieces * prows, half)
+    rel_parts = rel_parts.reshape(2, pieces, prows, half)
     return pl.pallas_call(
         functools.partial(store_kernel, rels),
         out_shape=(grad, grad, jax.ShapeDtypeStruct((rels, width), F32)),
@@ -502,7 +520,8 @@
         out_specs=(anywhere,) * 3,
         scratch_shapes=[
             vmem(rel_parts.shape, BF16), vmem((rels, width), F32),
-            vmem((ent, width), F32), vmem((ent, width), F32), dma((3,)), dma((3,)),
+            vmem((ent, width), F32), vmem((ent, width), F32),
+            dma((2 + 2 * pieces,)), dma((2 + pieces,)),
         ],
         compiler_params=pltpu.CompilerParams(vmem_limit_bytes=56 * 1024 * 1024),
     )(grad_src, grad_dst, rel_parts)

time: 62.1 us -> 59.4 us (0.957)
  Pallas kernels: 61.1 us -> 58.3 us
    pallas_call x1, Pallas kernels: 58.4 us -> 55.8 us  [body(): pl.pallas_call(functools.partial(kernel, nz, rels, rows_mm, pieces), out_...]
where the time goes in v6:
time: 59.4 us; the launch traced here: 59.1 us
  Pallas kernels  58.3 us (98%)
  between operations  0.8 us (1%)
    pallas_call x1, Pallas kernels, body(): pl.pallas_call(functools.partial(kernel, nz, rels, rows_mm, pieces), out_...  55.8 us
    pallas_call x1, Pallas kernels, body(): pl.pallas_call(functools.partial(store_kernel, rels), out_shape=(grad, gr...  2.52 us

profile of v6, /device:TPU:1, one launch (start us, length us, event | category | flops | bytes accessed | tf_op | source)
XLA Modules:
  0.0 59.1 jit_solution(3076165368382011784)
XLA Ops:
  0.6 55.8 %shard_map.103 = (f32[512,256]{1,0:T(8,128)}, f32[512,256]{1,0:T(8,128)}, bf16[2,3,4,8,16,128]{5,4,3,2,1,0:T(8,128)(2,1)}) custom-call(bf16[512,256]{1,0:T(8,128)(2,1)} %src_hbm.1, bf16[512,256]{1,0:T(8,128)(2,1)} %dst_hbm.1, f32[1345,256]{1,0:T(8,128)} %rel_hbm.1, s32[4,512]{1,0:T(4,128)} %bitcast.7, s32[4,512]{1,0:T(4,128)} %bitcast.8, s32[4,512]{1,0:T(4,128)} %bitcast.9, ...), custom_call_target="tpu_custom_call" | custom-call | tf_op jit(solution)/shard_map/pallas_call | solution.py:503
  56.4 2.5 %shard_map.104 = (f32[512,256]{1,0:T(8,128)}, f32[512,256]{1,0:T(8,128)}, f32[1345,256]{1,0:T(8,128)}) custom-call(f32[512,256]{1,0:T(8,128)} %get-tuple-element.6.gs_in, f32[512,256]{1,0:T(8,128)} %get-tuple-element.7.gd_in, bf16[2,3,512,128]{3,2,1,0:T(8,128)(2,1)} %bitcast.6), custom_call_target="tpu_custom_call" | custom-call | tf_op jit(solution)/shard_map/pallas_call | solution.py:516

commit v7 on v6

--- a/solution.py
+++ b/solution.py
@@ -276,27 +276,6 @@
     def rows_at(i, size):
         return pl.ds(pl.multiple_of(i * size, size), size)
 
-    for w in (2, 3):
-        gw[w] = nt(pulls[w], qt[w])
-    ga_send[...] = (gw[3] + jnp.where(even, gw[2], 0.0)).astype(BF16)
-    pair_copy = remote(ga_send, ga_recv, g_send.at[1], g_recv.at[1], sib)
-    pair_copy.start()
-    last = nt(ohs[:, lanes(3)], back_v[:, lanes(3)])
-    gs_send[...] = last.astype(BF16)
-    src_copy = remote(gs_send, gs_recv, g_send.at[2], g_recv.at[2], (grp, nxt))
-
-    @pl.when(even)
-    def _():
-        src_copy.start()
-
-    gw[1] = nt(pulls[1], qt[1])
-    gb_send[...] = gw[1].astype(BF16)
-    home_copy = remote(gb_send, gb_recv, g_send.at[0], g_recv.at[0], sib)
-
-    @pl.when(core == 1)
-    def _():
-        home_copy.start()
-
     for p in range(pieces):
         arrived(half_recv.at[p], s_recv.at[p])
         xs[p] = (gr[core, p * prows:(p + 1) * prows, :] + half_recv[p]).astype(BF16)
@@ -305,10 +284,27 @@
                 xs.at[p, rows_at(i, xrows)], x_recv.at[p, k - 1], xs_send.at[p], xs_recv.at[p], at_x(i)
             ).start()
 
-    arrived(ga_recv, g_recv.at[1])
-    gh_send[...] = (gw[1 + core] + ga_recv[...].astype(F32)).astype(BF16)
+    last = nt(ohs[:, lanes(3)], back_v[:, lanes(3)])
+    gs_send[...] = last.astype(BF16)
+    src_copy = remote(gs_send, gs_recv, g_send.at[2], g_recv.at[2], (grp, nxt))
+
+    @pl.when(even)
+    def _():
+        src_copy.start()
+
+    for w in range(4):
+        gw[w] = nt(pulls[w], qt[w])
+    ga_send[...] = (gw[3] + jnp.where(even, gw[2], 0.0)).astype(BF16)
+    pair_copy = remote(ga_send, ga_recv, g_send.at[1], g_recv.at[1], sib)
+    pair_copy.start()
     sent.append(pair_copy)
-    gw[0] = nt(pulls[0], qt[0])
+    gb_send[...] = gw[1].astype(BF16)
+    home_copy = remote(gb_send, gb_recv, g_send.at[0], g_recv.at[0], sib)
+
+    @pl.when(core == 1)
+    def _():
+        home_copy.start()
+
     own_slots = pl.ds(0, 3 * ent)
     gs[...] = nt(ohs[:, own_slots], back_v[:, own_slots])
 
@@ -326,6 +322,9 @@
             remote(
                 ys.at[p, rows_at(i, yrows)], y_recv.at[p, k - 1], ys_send.at[p], ys_recv.at[p], at_y(i)
             ).start()
+
+    arrived(ga_recv, g_recv.at[1])
+    gh_send[...] = (gw[1 + core] + ga_recv[...].astype(F32)).astype(BF16)
 
     for p in range(pieces):
         total = ys[p, rows_at(y, yrows), :].astype(F32)

time: 59.4 us -> 58.8 us (0.990)
  no operation moved by 1% of the time
where the time goes in v7:
time: 58.8 us; the launch traced here: 58.7 us
  Pallas kernels  57.9 us (98%)
  between operations  0.8 us (1%)
    pallas_call x1, Pallas kernels, body(): pl.pallas_call(functools.partial(kernel, nz, rels, rows_mm, pieces), out_...  55.3 us
    pallas_call x1, Pallas kernels, body(): pl.pallas_call(functools.partial(store_kernel, rels), out_shape=(grad, gr...  2.52 us

profile of v7, /device:TPU:1, one launch (start us, length us, event | category | flops | bytes accessed | tf_op | source)
XLA Modules:
  0.0 58.7 jit_solution(1087262996963537536)
XLA Ops:
  0.6 55.3 %shard_map.103 = (f32[512,256]{1,0:T(8,128)}, f32[512,256]{1,0:T(8,128)}, bf16[2,3,4,8,16,128]{5,4,3,2,1,0:T(8,128)(2,1)}) custom-call(bf16[512,256]{1,0:T(8,128)(2,1)} %src_hbm.1, bf16[512,256]{1,0:T(8,128)(2,1)} %dst_hbm.1, f32[1345,256]{1,0:T(8,128)} %rel_hbm.1, s32[4,512]{1,0:T(4,128)} %bitcast.7, s32[4,512]{1,0:T(4,128)} %bitcast.8, s32[4,512]{1,0:T(4,128)} %bitcast.9, ...), custom_call_target="tpu_custom_call" | custom-call | tf_op jit(solution)/shard_map/pallas_call | solution.py:502
  56.0 2.5 %shard_map.104 = (f32[512,256]{1,0:T(8,128)}, f32[512,256]{1,0:T(8,128)}, f32[1345,256]{1,0:T(8,128)}) custom-call(f32[512,256]{1,0:T(8,128)} %get-tuple-element.6.gs_in, f32[512,256]{1,0:T(8,128)} %get-tuple-element.7.gd_in, bf16[2,3,512,128]{3,2,1,0:T(8,128)(2,1)} %bitcast.6), custom_call_target="tpu_custom_call" | custom-call | tf_op jit(solution)/shard_map/pallas_call | solution.py:515

commit v8 on v7

--- a/solution.py
+++ b/solution.py
@@ -230,11 +230,11 @@
     src_t[...] = src_v[...].T
 
     gather(0)
+    gather(1)
     finish(0, 0)
+    gather(2)
     for p in range(pieces):
         grow(p, 0, 1)
-    gather(1)
-    gather(2)
 
     @pl.when(even)
     def _():

time: 58.8 us -> 58.9 us (level)
  no operation moved by 1% of the time
where the time goes in v8:
time: 58.9 us; the launch traced here: 58.8 us
  Pallas kernels  58 us (98%)
  between operations  0.8 us (1%)
    pallas_call x1, Pallas kernels, body(): pl.pallas_call(functools.partial(kernel, nz, rels, rows_mm, pieces), out_...  55.4 us
    pallas_call x1, Pallas kernels, body(): pl.pallas_call(functools.partial(store_kernel, rels), out_shape=(grad, gr...  2.52 us

profile of v8, /device:TPU:1, one launch (start us, length us, event | category | flops | bytes accessed | tf_op | source)
XLA Modules:
  0.0 58.8 jit_solution(14372121087782096376)
XLA Ops:
  0.6 55.4 %shard_map.103 = (f32[512,256]{1,0:T(8,128)}, f32[512,256]{1,0:T(8,128)}, bf16[2,3,4,8,16,128]{5,4,3,2,1,0:T(8,128)(2,1)}) custom-call(bf16[512,256]{1,0:T(8,128)(2,1)} %src_hbm.1, bf16[512,256]{1,0:T(8,128)(2,1)} %dst_hbm.1, f32[1345,256]{1,0:T(8,128)} %rel_hbm.1, s32[4,512]{1,0:T(4,128)} %bitcast.7, s32[4,512]{1,0:T(4,128)} %bitcast.8, s32[4,512]{1,0:T(4,128)} %bitcast.9, ...), custom_call_target="tpu_custom_call" | custom-call | tf_op jit(solution)/shard_map/pallas_call | solution.py:502
  56.1 2.5 %shard_map.104 = (f32[512,256]{1,0:T(8,128)}, f32[512,256]{1,0:T(8,128)}, f32[1345,256]{1,0:T(8,128)}) custom-call(f32[512,256]{1,0:T(8,128)} %get-tuple-element.6.gs_in, f32[512,256]{1,0:T(8,128)} %get-tuple-element.7.gd_in, bf16[2,3,512,128]{3,2,1,0:T(8,128)(2,1)} %bitcast.6), custom_call_target="tpu_custom_call" | custom-call | tf_op jit(solution)/shard_map/pallas_call | solution.py:515
